TPU v7x, 32 devices: a whole 2x2x4 slice. The times are simulated.
32 devices in a mesh: scene: 16 (over z, y, x), veh: 2 (over core).
Axes of the slice: x: 2, y: 2, z: 4, core: 2. Of those that a mesh axis runs over, the one named last changes fastest.
Arguments:
- features: bfloat16 [16, 4, 256, 16, 128], P('scene', 'veh'), may hold values from -64 to 64
- counts: int32 [16], P('scene'), may hold values from 2 to 4, as said below
- ego_ids: int32 [16], P('scene'), may hold values from 0 to 3, as said below
- req_tiles: int32 [16, 4, 2], P('scene', 'veh'), may hold values from 0 to 3, as said below
- req_count: int32 [16, 4], P('scene', 'veh'), may hold values from 1 to 2, as said below
- ego_embed: bfloat16 [256], replicated, may hold values from -8 to 8
- enc_weight: bfloat16 [9, 256, 256], replicated, may hold values from -0.125 to 0.125
- post_weight: bfloat16 [9, 256, 256], replicated, may hold values from -0.125 to 0.125
- cotangent: bfloat16 [16, 256, 16, 128], P('scene', None, 'veh'), may hold values from -6 to 6
Outputs:
- refined: bfloat16 [16, 256, 16, 128], P('scene', None, 'veh')
- feature_grad: float32 [16, 4, 256, 16, 128], P('scene', 'veh')
- enc_grad: float32 [9, 256, 256], replicated
- post_grad: float32 [9, 256, 256], replicated
- embed_grad: float32 [256], replicated
Inputs may be any that keep to these rules, and one draw needn't show every extreme that they name: `counts`: some scene has all 4 vehicles. `ego_ids`: the ego is one of the scene's present vehicles; in some scene with all 4 vehicles in which the ego asks 2 tiles of every other vehicle, the ego is the last vehicle. `req_tiles`: the 2 tile ids of one vehicle are distinct. `req_count`: the ego's own entry and those of vehicles at or beyond the count are not used; in some scene with all 4 vehicles the ego asks 2 tiles of every other vehicle.
All inputs are finite; a program needn't handle non-finite values.
Results may differ from a plain program's by a relative error of at most 0.012.
The roundings to bfloat16 on the way count: a program that leaves them out, or rounds other values in their place, can miss the bound.
Values may be sent and summed in bfloat16 or wider, within the bound.
A program may use at most 192 MiB of HBM per device.

v0:
```python
import jax
import jax.numpy as jnp
from jax import lax
from jax.experimental import pallas as pl
from jax.experimental.pallas import tpu as pltpu
from jax.sharding import PartitionSpec as P

TILE = 32
KMAX = 2
F32 = jnp.float32
BF16 = jnp.bfloat16
LANES = 128
CHUNK = 512
VMEM_LIMIT = 56 * 1024 * 1024


def sigmoid(z):
    return 1.0 / (1.0 + jnp.exp(-z))


def silu_slope(z):
    sig = sigmoid(z)
    return sig * (1.0 + z * (1.0 - sig))


def clear_pads(taps_ref, cells):
    rows = taps_ref.shape[0]
    taps_ref[:, : 2 * LANES] = jnp.zeros((rows, 2 * LANES), BF16)
    taps_ref[:, 2 * LANES + cells :] = jnp.zeros((rows, 2 * LANES), BF16)


def put_row(taps_ref, r, row):
    channels = row.shape[0]
    lane = lax.broadcasted_iota(jnp.int32, row.shape, 1)
    at = slice((r + 2) * LANES, (r + 3) * LANES)
    left = jnp.where(lane >= 2, pltpu.roll(row, 2, 1), 0.0)
    right = jnp.where(lane < LANES - 2, pltpu.roll(row, LANES - 2, 1), 0.0)
    taps_ref[:channels, at] = left.astype(BF16)
    taps_ref[channels : 2 * channels, at] = row.astype(BF16)
    taps_ref[2 * channels :, at] = right.astype(BF16)


def turn_weight(w_ref, wt_ref):
    channels = w_ref.shape[1]
    for t in range(9):
        at = slice(t * channels, (t + 1) * channels)
        wt_ref[:, at] = w_ref[at, :].T


def flip_weight(w_ref, wb_ref):
    channels = w_ref.shape[1]
    for t in range(9):
        wb_ref[:, t * channels : (t + 1) * channels] = w_ref[
            (8 - t) * channels : (9 - t) * channels, :
        ]


def conv_chunk(w_ref, taps_ref, j):
    depth = taps_ref.shape[0]
    total = None
    for a in range(3):
        part = jnp.dot(
            w_ref[:, a * depth : (a + 1) * depth],
            taps_ref[:, a * 2 * LANES + j * CHUNK : a * 2 * LANES + (j + 1) * CHUNK],
            preferred_element_type=F32,
        )
        total = part if total is None else total + part
    return total


def dot_nt(left, right, precision=None):
    return lax.dot_general(
        left, right, (((1,), (1,)), ((), ())), preferred_element_type=F32, precision=precision
    )


def load_map(x_ref, wide_ref, taps_ref, rows):
    channels = taps_ref.shape[0] // 3
    wide_ref[...] = x_ref[0].astype(F32)
    clear_pads(taps_ref, rows * LANES)
    for r in range(rows):
        put_row(taps_ref, r, wide_ref[pl.ds(r, channels, stride=rows), :])


def encode_kernel(x_ref, w_ref, pre_ref, enc_ref, wide_ref, taps_ref, wt_ref):
    channels = w_ref.shape[1]
    cells = pre_ref.shape[-1]
    rows = cells // LANES

    @pl.when(pl.program_id(0) == 0)
    def _():
        turn_weight(w_ref, wt_ref)

    load_map(x_ref, wide_ref, taps_ref, rows)
    for j in range(cells // CHUNK):
        at = slice(j * CHUNK, (j + 1) * CHUNK)
        pre = conv_chunk(wt_ref, taps_ref, j)
        here = taps_ref[channels : 2 * channels, 2 * LANES + j * CHUNK : 2 * LANES + (j + 1) * CHUNK]
        pre_ref[0, :, at] = pre
        enc_ref[0, :, at] = (here.astype(F32) + pre * sigmoid(pre)).astype(BF16)


def encode(x, weight):
    veh, deep, _ = x.shape
    channels = weight.shape[1]
    cells = deep // channels * LANES
    return pl.pallas_call(
        encode_kernel,
        grid=(veh,),
        out_shape=(
            jax.ShapeDtypeStruct((veh, channels, cells), F32),
            jax.ShapeDtypeStruct((veh, channels, cells), BF16),
        ),
        in_specs=[
            pl.BlockSpec((1, deep, LANES), lambda v: (v, 0, 0)),
            pl.BlockSpec((9 * channels, channels), lambda v: (0, 0)),
        ],
        out_specs=(
            pl.BlockSpec((1, channels, cells), lambda v: (v, 0, 0)),
            pl.BlockSpec((1, channels, cells), lambda v: (v, 0, 0)),
        ),
        scratch_shapes=[
            pltpu.VMEM((deep, LANES), F32),
            pltpu.VMEM((3 * channels, cells + 4 * LANES), BF16),
            pltpu.VMEM((channels, 9 * channels), BF16),
        ],
        compiler_params=pltpu.CompilerParams(vmem_limit_bytes=VMEM_LIMIT),
        cost_estimate=pl.CostEstimate(
            flops=2 * veh * 9 * channels * channels * cells,
            bytes_accessed=veh * channels * cells * 8,
            transcendentals=veh * channels * cells,
        ),
        name="encode",
    )(x, weight)


def post_kernel(
    ids_ref, enc_ref, live_ref, embed_ref, cot_ref, w_ref,
    refined_ref, grad_ref, eg_ref,
    wide_ref, cotw_ref, taps_ref, slope_ref, wt_ref, out_ref, weights_ref, jg_ref,
):
    vehicles, channels, cells = enc_ref.shape
    rows = cells // LANES
    half = rows // 2
    local = eg_ref.shape[0]
    ego, me = ids_ref[0], ids_ref[1]
    inv = 1.0 / channels
    turn_weight(w_ref, wt_ref)
    clear_pads(taps_ref, cells)
    clear_pads(slope_ref, cells)
    embed = embed_ref[...]

    def colsum(x):
        return jnp.sum(x, axis=0, keepdims=True)

    for r in range(rows):
        at = slice(r * LANES, (r + 1) * LANES)
        query = enc_ref[ego, :, at].astype(F32)
        score_self = colsum(query * (query + embed)) * inv
        scores, top = [], score_self
        for v in range(vehicles):
            score = colsum(query * enc_ref[v, :, at].astype(F32)) * inv
            live = live_ref[v : v + 1, :] > 0.5
            top = jnp.maximum(top, jnp.where(live, score, -jnp.inf))
            scores.append(score)
        exps = [jnp.exp(score_self - top)]
        for v in range(vehicles):
            live = live_ref[v : v + 1, :] > 0.5
            exps.append(jnp.where(live, jnp.exp(jnp.minimum(scores[v] - top, 0.0)), 0.0))
        total = exps[0]
        for e in exps[1:]:
            total = total + e
        scale = 1.0 / total
        joined = exps[0] * scale * query
        weights_ref[0, :, at] = exps[0] * scale
        for v in range(vehicles):
            weight = exps[v + 1] * scale
            weights_ref[v + 1, :, at] = weight
            joined = joined + weight * enc_ref[v, :, at].astype(F32)
        put_row(taps_ref, r, joined.astype(BF16).astype(F32))

    for h in range(2):
        wide_ref[...] = cot_ref[h].astype(F32)
        for r in range(half):
            at = slice((h * half + r) * LANES, (h * half + r + 1) * LANES)
            cotw_ref[:, at] = wide_ref[pl.ds(r, channels, stride=half), :]

    for j in range(cells // CHUNK):
        at = slice(j * CHUNK, (j + 1) * CHUNK)
        pre = conv_chunk(wt_ref, taps_ref, j)
        sig = sigmoid(pre)
        joined = taps_ref[
            channels : 2 * channels, 2 * LANES + j * CHUNK : 2 * LANES + (j + 1) * CHUNK
        ].astype(F32)
        out_ref[:, at] = joined + pre * sig
        slope = cotw_ref[:, at] * (sig * (1.0 + pre * (1.0 - sig)))
        slope = slope.astype(BF16).astype(F32)
        for k in range(CHUNK // LANES):
            put_row(slope_ref, j * (CHUNK // LANES) + k, slope[:, k * LANES : (k + 1) * LANES])

    for k in range(half):
        at = pl.ds(pl.multiple_of((me * half + k) * LANES, LANES), LANES)
        wide_ref[pl.ds(k, channels, stride=half), :] = out_ref[:, at]
    refined_ref[...] = wide_ref[...].astype(BF16)

    flip_weight(w_ref, wt_ref)
    for j in range(cells // CHUNK):
        at = slice(j * CHUNK, (j + 1) * CHUNK)
        jg_ref[:, at] = conv_chunk(wt_ref, slope_ref, j) + cotw_ref[:, at]

    base = me * half * LANES
    slope_half = slope_ref[
        channels : 2 * channels, pl.ds(pl.multiple_of(base + 2 * LANES, LANES), half * LANES)
    ]
    for a in range(3):
        depth = 3 * channels
        at = pl.ds(pl.multiple_of(base + a * 2 * LANES, LANES), half * LANES)
        grad_ref[a * depth : (a + 1) * depth, :] = dot_nt(taps_ref[:, at], slope_half).astype(BF16)

    acc = jnp.zeros((channels, LANES), F32)
    for r in range(rows):
        at = slice(r * LANES, (r + 1) * LANES)
        query = enc_ref[ego, :, at].astype(F32)
        jg = jg_ref[:, at]
        w_self = weights_ref[0, :, at]
        dot_self = colsum(jg * query)
        mean = w_self * dot_self
        dots = []
        for v in range(vehicles):
            dot = colsum(jg * enc_ref[v, :, at].astype(F32))
            mean = mean + weights_ref[v + 1, :, at] * dot
            dots.append(dot)
        slope_self = w_self * (dot_self - mean)
        ego_sum = slope_self * (2.0 * query + embed)
        for v in range(vehicles):
            slope_v = weights_ref[v + 1, :, at] * (dots[v] - mean)
            weights_ref[8 + v, :, at] = slope_v
            ego_sum = ego_sum + slope_v * enc_ref[v, :, at].astype(F32)
        ego_term = w_self * jg + ego_sum * inv
        for v in range(local):
            veh = me * local + v
            weight_v = weights_ref[veh + 1, :, at]
            slope_v = weights_ref[veh + 8, :, at]
            part = weight_v * jg + (slope_v * inv) * query
            eg_ref[v, :, at] = jnp.where(veh == ego, ego_term, part).astype(BF16)
        mine = jnp.where(me == r // half, inv, 0.0)
        acc = acc + (slope_self * mine) * query
    row = dot_nt(jnp.ones((16, LANES), F32), acc, precision=lax.Precision.HIGHEST)
    grad_ref[9 * channels :, :] = row.astype(BF16)


def post(ids, enc, live, embed, cot, weight, local):
    vehicles, channels, cells = enc.shape
    vm = pl.BlockSpec(memory_space=pltpu.VMEM)
    deep = cot.shape[1]
    return pl.pallas_call(
        post_kernel,
        out_shape=(
            jax.ShapeDtypeStruct((deep, LANES), BF16),
            jax.ShapeDtypeStruct((9 * channels + 16, channels), BF16),
            jax.ShapeDtypeStruct((local, channels, cells), BF16),
        ),
        in_specs=[pl.BlockSpec(memory_space=pltpu.SMEM)] + [vm] * 5,
        out_specs=(vm, vm, vm),
        scratch_shapes=[
            pltpu.VMEM((deep, LANES), F32),
            pltpu.VMEM((channels, cells), F32),
            pltpu.VMEM((3 * channels, cells + 4 * LANES), BF16),
            pltpu.VMEM((3 * channels, cells + 4 * LANES), BF16),
            pltpu.VMEM((channels, 9 * channels), BF16),
            pltpu.VMEM((channels, cells), F32),
            pltpu.VMEM((16, 1, cells), F32),
            pltpu.VMEM((channels, cells), F32),
        ],
        compiler_params=pltpu.CompilerParams(vmem_limit_bytes=VMEM_LIMIT),
        cost_estimate=pl.CostEstimate(
            flops=5 * 9 * channels * channels * cells,
            bytes_accessed=16 * channels * cells,
            transcendentals=channels * cells,
        ),
        name="post",
    )(ids, enc, live, embed, cot, weight)


def back_kernel(
    x_ref, pre_ref, eg_ref, w_ref, fg_ref, grad_ref, wide_ref, taps_ref, slope_ref, wb_ref, acc_ref
):
    channels = w_ref.shape[1]
    cells = pre_ref.shape[-1]
    rows = cells // LANES
    depth = 3 * channels
    first = pl.program_id(0) == 0

    @pl.when(first)
    def _():
        flip_weight(w_ref, wb_ref)
        acc_ref[...] = jnp.zeros_like(acc_ref)

    load_map(x_ref, wide_ref, taps_ref, rows)
    clear_pads(slope_ref, cells)
    for r in range(rows):
        at = slice(r * LANES, (r + 1) * LANES)
        slope = eg_ref[0, :, at].astype(F32) * silu_slope(pre_ref[0, :, at])
        put_row(slope_ref, r, slope.astype(BF16).astype(F32))
    here = slope_ref[channels : 2 * channels, 2 * LANES : 2 * LANES + cells]
    for a in range(3):
        acc_ref[a * depth : (a + 1) * depth, :] += dot_nt(
            taps_ref[:, a * 2 * LANES : a * 2 * LANES + cells], here
        )

    @pl.when(pl.program_id(0) == pl.num_programs(0) - 1)
    def _():
        grad_ref[...] = acc_ref[...].astype(BF16)

    for j in range(cells // CHUNK):
        back = conv_chunk(wb_ref, slope_ref, j)
        for k in range(CHUNK // LANES):
            r = j * (CHUNK // LANES) + k
            fg_ref[0, pl.ds(r, channels, stride=rows), :] = back[
                :, k * LANES : (k + 1) * LANES
            ] + eg_ref[0, :, r * LANES : (r + 1) * LANES].astype(F32)


def back(x, pre, eg, weight):
    veh, channels, cells = pre.shape
    deep = x.shape[1]
    return pl.pallas_call(
        back_kernel,
        grid=(veh,),
        out_shape=(
            jax.ShapeDtypeStruct((veh, deep, LANES), F32),
            jax.ShapeDtypeStruct((9 * channels, channels), BF16),
        ),
        in_specs=[
            pl.BlockSpec((1, deep, LANES), lambda v: (v, 0, 0)),
            pl.BlockSpec((1, channels, cells), lambda v: (v, 0, 0)),
            pl.BlockSpec((1, channels, cells), lambda v: (v, 0, 0)),
            pl.BlockSpec((9 * channels, channels), lambda v: (0, 0)),
        ],
        out_specs=(
            pl.BlockSpec((1, deep, LANES), lambda v: (v, 0, 0)),
            pl.BlockSpec((9 * channels, channels), lambda v: (0, 0)),
        ),
        scratch_shapes=[
            pltpu.VMEM((deep, LANES), F32),
            pltpu.VMEM((3 * channels, cells + 4 * LANES), BF16),
            pltpu.VMEM((3 * channels, cells + 4 * LANES), BF16),
            pltpu.VMEM((channels, 9 * channels), BF16),
            pltpu.VMEM((9 * channels, channels), F32),
        ],
        compiler_params=pltpu.CompilerParams(vmem_limit_bytes=VMEM_LIMIT),
        cost_estimate=pl.CostEstimate(
            flops=4 * veh * 9 * channels * channels * cells,
            bytes_accessed=veh * channels * cells * 12,
            transcendentals=veh * channels * cells,
        ),
        name="back",
    )(x, pre, eg, weight)


def body(
    features, counts, ego_ids, req_tiles, req_count, ego_embed, enc_weight, post_weight, cotangent
):
    batch, local, channels, rows, breadth = features.shape
    me = lax.axis_index("veh")
    veh_here = me * local + jnp.arange(local)
    present = (veh_here < counts[0]) & (veh_here != ego_ids[0])
    live_count = jnp.where(present, req_count[0], 0)
    asked = (req_tiles[0][:, :, None] == (jnp.arange(breadth) // TILE)[None, None, :]) & (
        jnp.arange(KMAX)[None, :, None] < live_count[:, None, None]
    )
    live = jnp.sum(asked.astype(F32), axis=1)
    live = lax.all_gather(live, "veh", axis=0, tiled=True)
    half = cotangent.shape[2]
    cot = lax.all_gather(cotangent.reshape(1, channels * half, breadth), "veh", axis=0, tiled=True)
    x = features.reshape(local, channels * rows, breadth)
    enc_w = enc_weight.reshape(9 * channels, channels)
    post_w = post_weight.reshape(9 * channels, channels)
    pre, encoded = encode(x, enc_w)
    enc_all = lax.all_gather(encoded, "veh", axis=0, tiled=True)
    ids = jnp.stack([ego_ids[0], me]).astype(jnp.int32)
    embed = jnp.broadcast_to(ego_embed.astype(F32)[:, None], (channels, LANES))
    refined, post_part, eg = post(ids, enc_all, live, embed, cot, post_w, local)
    post_sum = lax.psum(post_part, ("scene", "veh")).astype(F32)
    fg, enc_part = back(x, pre, eg, enc_w)
    enc_sum = lax.psum(enc_part, ("scene", "veh")).astype(F32)
    return (
        refined.reshape(batch, channels, half, breadth),
        fg.reshape(features.shape),
        enc_sum.reshape(enc_weight.shape),
        post_sum[: 9 * channels].reshape(post_weight.shape),
        post_sum[9 * channels],
    )


def solution(mesh):
    in_specs = (
        P("scene", "veh", None, None, None),
        P("scene"),
        P("scene"),
        P("scene", "veh", None),
        P("scene", "veh"),
        P(),
        P(),
        P(),
        P("scene", None, "veh", None),
    )
    out_specs = (P("scene", None, "veh", None), P("scene", "veh", None, None, None), P(), P(), P())
    return jax.shard_map(body, mesh=mesh, in_specs=in_specs, out_specs=out_specs, check_vma=False)
```

profile of v0, /device:TPU:0, one launch (start us, length us, event | category | flops | bytes accessed | tf_op | source)
XLA Modules:
  0.0 228.9 jit_solution(1874457628520091366)
XLA Ops:
  7.2 0.0 all-gather.6.cloned.1.call-start
  7.2 0.7 all-gather.6.cloned.1.call-update
  7.9 0.0 all-gather.4.cloned.1.call-start
  7.9 10.3 %encode.1 = (f32[2,256,2048]{2,1,0:T(8,128)}, bf16[2,256,2048]{2,1,0:T(8,128)(2,1)}) custom-call(bf16[2,4096,128]{2,1,0:T(8,128)(2,1)} %bitcast.26, bf16[2304,256]{1,0:T(8,128)(2,1)} %bitcast.29), custom_call_target="tpu_custom_call" | custom-call | flops 4831838208 | bytes 8388608 | tf_op jit(solution)/shard_map/encode/pallas_call | solution.py:107
  18.2 0.0 copy-start.3
  18.2 0.0 copy-start.1
  18.2 0.0 copy-start.2
  18.2 0.0 all-gather.4.cloned.1.call-update
  18.3 0.0 all-reduce.3.cloned.1.call-start
  19.6 0.0 copy-done.3
  19.7 0.1 iota_compare_fusion
  19.7 0.0 copy-done.1
  19.7 0.1 fusion
  19.8 2.2 all-gather
  22.0 0.6 pad_add_fusion.ids_ref
  22.7 0.0 all-gather.6.cloned.1.call-done.cot_ref
  22.7 15.6 %all-gather.4.cloned.1.call-done.enc_ref = bf16[4,256,2048]{2,1,0:T(8,128)(2,1)} async-done(((bf16[2,256,2048]{2,1,0:T(8,128)(2,1)}), bf16[4,256,2048]{2,1,0:T(8,128)(2,1)}) %all-gather.4.cloned.1.call-update) | async-done | bytes 4194320 | tf_op jit(solution)/shard_map/all_gather | solution.py:380
  38.3 0.0 copy-done.2
  38.3 0.8 broadcast_in_dim.7.embed_ref
  39.1 18.3 %post.1 = (bf16[2048,128]{1,0:T(8,128)(2,1)}, bf16[2320,256]{1,0:T(8,128)(2,1)}, bf16[2,256,2048]{2,1,0:T(8,128)(2,1)}) custom-call(s32[2]{0:T(128)} %pad_add_fusion.ids_ref, bf16[4,256,2048]{2,1,0:T(8,128)(2,1)} %all-gather.4.cloned.1.call-done.enc_ref, f32[4,128]{1,0:T(4,128)} %bitcast.23, f32[256,128]{1,0:T(8,128)} %broadcast_in_dim.7.embed_ref, ...), custom_call_target="tpu_custom_call" | custom-call | flops 6039797760 | bytes 8388608 | tf_op jit(solution)/shard_map/post/pallas_call | solution.py:256
  57.4 22.9 %back.1 = (f32[2,4096,128]{2,1,0:T(8,128)}, bf16[2304,256]{1,0:T(8,128)(2,1)}) custom-call(bf16[2,4096,128]{2,1,0:T(8,128)(2,1)} %bitcast.27, f32[2,256,2048]{2,1,0:T(8,128)} %get-tuple-element.14.pre_ref, bf16[2,256,2048]{2,1,0:T(8,128)(2,1)} %get-tuple-element.15.eg_ref, bf16[2304,256]{1,0:T(8,128)(2,1)} %bitcast.30), custom_call_target="tpu_custom_call" | custom-call | flops 9663676416 | bytes 12582912 | tf_op jit(solution)/shard_map/back/pallas_call | solution.py:327
  80.3 0.0 all-reduce.3.cloned.1.call-update
  80.3 136.2 %all-reduce.3.cloned.1.call-done = (bf16[9,256,256]{2,1,0:T(8,128)(2,1)}, bf16[2320,256]{1,0:T(8,128)(2,1)}) async-done(((bf16[9,256,256]{2,1,0:T(8,128)(2,1)}, bf16[2320,256]{1,0:T(8,128)(2,1)}), (bf16[9,256,256]{2,1,0:T(8,128)(2,1)}, bf16[2320,256]{1,0:T(8,128)(2,1)})) %all-reduce.3.cloned.1.call-update) | async-done | bytes 2367504 | tf_op jit(solution)/shard_map/psum | solution.py:386
  216.5 1.2 slice.9
  217.8 0.0 copy-start
  217.8 3.0 %slice.8 = f32[2304,256]{1,0:T(8,128)} slice(bf16[2320,256]{1,0:T(8,128)(2,1)} %get-tuple-element.20), slice={[0:2304], [0:256]} | slice | bytes 4718592 | tf_op jit(solution)/shard_map/slice | solution.py:391
  220.7 0.0 copy-done
  220.7 1.6 reshape.95
  (2 shorter events, 0.0 us)
Async XLA Ops:
  7.2 15.5 %all-gather.6.cloned.1.call-start = ((), (), s32[]{:S(2)}) async-start(), calls=%async_computation.1 | async-start | bytes 1572864 | tf_op jit(solution)/shard_map/all_gather | solution.py:375
  7.9 30.4 %all-gather.4.cloned.1.call-start = ((), (), s32[]{:S(2)}) async-start(), calls=%async_computation | async-start | bytes 6291456 | tf_op jit(solution)/shard_map/all_gather | solution.py:380
  18.2 1.4 copy-start.3
  18.2 1.5 copy-start.1
  18.2 20.1 %copy-start.2 = (bf16[256]{0:T(256)(128)(2,1)S(1)}, bf16[256]{0:T(256)(128)(2,1)}, u32[]{:S(2)}) copy-start(bf16[256]{0:T(256)(128)(2,1)} %param.14) | copy-start | bytes 1540
  18.3 198.2 %all-reduce.3.cloned.1.call-start = ((), (), s32[]{:S(2)}) async-start(), calls=%async_computation.2 | async-start | bytes 4734976 | tf_op jit(solution)/shard_map/psum | solution.py:386
  217.8 3.0 %copy-start = (bf16[9,256,256]{2,1,0:T(8,128)(2,1)S(1)}, bf16[9,256,256]{2,1,0:T(8,128)(2,1)}, u32[]{:S(2)}) copy-start(bf16[9,256,256]{2,1,0:T(8,128)(2,1)} %get-tuple-element.19) | copy-start | bytes 3538948
Sparse Core Ops, SparseCore 0:
  9.5 11.7 all-gather.5
  23.4 14.8 all-gather.3
  80.4 136.0 all-reduce.2
where the time goes:
time: 229 us
  waiting for transfers between devices  153 us (67%)
  Pallas kernels  51.5 us (22%)
  between operations  15.1 us (7%)
  local copies, waits for them, and re-layouts  4.97 us (2%)
  other arithmetic  2.44 us (1%)
    psum x1, waiting for transfers between devices, body(): enc_sum = lax.psum(enc_part, ('scene', 'veh')).astype(F32)  136 us
    pallas_call x1, Pallas kernels, back(): pl.pallas_call(back_kernel, grid=(veh,), out_shape=(jax.ShapeDtypeStruct(...  22.9 us
    pallas_call x1, Pallas kernels, post(): pl.pallas_call(post_kernel, out_shape=(jax.ShapeDtypeStruct((deep, LANES)...  18.3 us
    all_gather x1, waiting for transfers between devices, body(): enc_all = lax.all_gather(encoded, 'veh', axis=0, tiled=True)  15.6 us
    pallas_call x1, Pallas kernels, encode(): pl.pallas_call(encode_kernel, grid=(veh,), out_shape=(jax.ShapeDtypeStruc...  10.3 us
  transfers between devices with their start and end apart: 3, of which 2 were waited for; matrix products, arithmetic and copies ran while one was open for 0% of the time, Pallas kernels for 4%

commit v1 on v0

--- a/solution.py
+++ b/solution.py
@@ -358,6 +358,28 @@
     )(x, pre, eg, weight)
 
 
+def swap(x, axis, bit):
+    size = lax.axis_size(axis)
+    return lax.ppermute(x, axis, [(i, i ^ (1 << bit)) for i in range(size)])
+
+
+def sum_over_devices(part, order):
+    pad = -part.shape[0] % (1 << len(order))
+    total = jnp.pad(part, ((0, pad), (0, 0))).astype(F32)
+    for axis, bit in order:
+        half = total.shape[0] // 2
+        high = ((lax.axis_index(axis) >> bit) & 1) == 1
+        low_rows, high_rows = total[:half], total[half:]
+        sent = jnp.where(high, low_rows, high_rows).astype(BF16)
+        total = jnp.where(high, high_rows, low_rows) + swap(sent, axis, bit).astype(F32)
+    whole = total.astype(BF16)
+    for axis, bit in reversed(order):
+        high = ((lax.axis_index(axis) >> bit) & 1) == 1
+        other = swap(whole, axis, bit)
+        whole = jnp.concatenate([jnp.where(high, other, whole), jnp.where(high, whole, other)], axis=0)
+    return whole[: part.shape[0]].astype(F32)
+
+
 def body(
     features, counts, ego_ids, req_tiles, req_count, ego_embed, enc_weight, post_weight, cotangent
 ):
@@ -381,9 +403,16 @@
     ids = jnp.stack([ego_ids[0], me]).astype(jnp.int32)
     embed = jnp.broadcast_to(ego_embed.astype(F32)[:, None], (channels, LANES))
     refined, post_part, eg = post(ids, enc_all, live, embed, cot, post_w, local)
-    post_sum = lax.psum(post_part, ("scene", "veh")).astype(F32)
+    scene_bits = [("scene", b) for b in range(lax.axis_size("scene").bit_length() - 1)]
+    veh_bits = [("veh", b) for b in range(lax.axis_size("veh").bit_length() - 1)]
+    one = veh_bits + scene_bits
+    two = veh_bits + scene_bits[1:2] + scene_bits[:1] + scene_bits[2:]
+    post_sum = sum_over_devices(post_part, two)
     fg, enc_part = back(x, pre, eg, enc_w)
-    enc_sum = lax.psum(enc_part, ("scene", "veh")).astype(F32)
+    cut = enc_part.shape[0] // 2
+    enc_sum = jnp.concatenate(
+        [sum_over_devices(enc_part[:cut], one), sum_over_devices(enc_part[cut:], two)], axis=0
+    )
     return (
         refined.reshape(batch, channels, half, breadth),
         fg.reshape(features.shape),

time: 229 us -> 171 us (0.75)
  waiting for transfers between devices: 153 us -> 52.3 us
  starting transfers between devices: 0.12 us -> 39 us
  other arithmetic: 2.44 us -> 7.3 us
    psum x1 -> x0, waiting for transfers between devices: 136 us -> none  [body(): enc_sum = lax.psum(enc_part, ('scene', 'veh')).astype(F32)]
    ppermute x0 -> x30, starting transfers between devices: none -> 39 us  [swap(): return lax.ppermute(x, axis, [(i, i ^ 1 << bit) for i in range(size)])]
    ppermute x0 -> x30, waiting for transfers between devices: none -> 36 us  [swap(): return lax.ppermute(x, axis, [(i, i ^ 1 << bit) for i in range(size)])]
    convert_element_type x0 -> x21, other arithmetic: none -> 2.32 us  [the longest x2 1.6 us: sum_over_devices(): total = jnp.pad(part, ((0, pad), (0, 0))).astype(F32)]
  transfers between devices with their start and end apart: 3 -> 32, of which waited for: 2 -> 16; matrix products, arithmetic and copies ran while one was open for 0% -> 3% of each run, Pallas kernels for 4% -> 6%
where the time goes in v1:
time: 171 us
  waiting for transfers between devices  52.3 us (31%)
  Pallas kernels  51.5 us (30%)
  starting transfers between devices  39 us (23%)
  between operations  15.8 us (9%)
  other arithmetic  7.3 us (4%)
  local copies, waits for them, and re-layouts  2.83 us (2%)
  blocking collectives  2.23 us (1%)
    ppermute x30, starting transfers between devices, swap(): return lax.ppermute(x, axis, [(i, i ^ 1 << bit) for i in range(size)])  39 us
    ppermute x30, waiting for transfers between devices, swap(): return lax.ppermute(x, axis, [(i, i ^ 1 << bit) for i in range(size)])  36 us
    pallas_call x1, Pallas kernels, back(): pl.pallas_call(back_kernel, grid=(veh,), out_shape=(jax.ShapeDtypeStruct(...  22.9 us
    pallas_call x1, Pallas kernels, post(): pl.pallas_call(post_kernel, out_shape=(jax.ShapeDtypeStruct((deep, LANES)...  18.3 us
    all_gather x1, waiting for transfers between devices, body(): enc_all = lax.all_gather(encoded, 'veh', axis=0, tiled=True)  15.7 us
    pallas_call x1, Pallas kernels, encode(): pl.pallas_call(encode_kernel, grid=(veh,), out_shape=(jax.ShapeDtypeStruc...  10.3 us
  transfers between devices with their start and end apart: 32, of which 16 were waited for; matrix products, arithmetic and copies ran while one was open for 3% of the time, Pallas kernels for 6%

profile of v1, /device:TPU:0, one launch (start us, length us, event | category | flops | bytes accessed | tf_op | source)
XLA Modules:
  0.0 171.0 jit_solution(14756546207029596031)
XLA Ops:
  7.2 0.7 all-gather.6.cloned.1.call-update
  7.9 10.3 %encode.1 = (f32[2,256,2048]{2,1,0:T(8,128)}, bf16[2,256,2048]{2,1,0:T(8,128)(2,1)}) custom-call(bf16[2,4096,128]{2,1,0:T(8,128)(2,1)} %bitcast.27, bf16[2304,256]{1,0:T(8,128)(2,1)} %bitcast.30), custom_call_target="tpu_custom_call" | custom-call | flops 4831838208 | bytes 8388608 | tf_op jit(solution)/shard_map/encode/pallas_call | solution.py:107
  19.8 2.2 %all-gather = f32[2,2,128]{2,1,0:T(2,128)} all-gather(f32[1,2,128]{2,1,0:T(2,128)S(1)} %bitcast.23), channel_id=1, replica_groups=mesh['scene'=16,'veh'=2] {'veh'}, dimensions={0}, use_global_device_ids=true | all-gather | bytes 3072 | tf_op jit(solution)/shard_map/all_gather | solution.py:395
  22.0 0.6 pad_add_fusion.ids_ref
  22.6 15.7 %all-gather.4.cloned.1.call-done.enc_ref = bf16[4,256,2048]{2,1,0:T(8,128)(2,1)} async-done(((bf16[2,256,2048]{2,1,0:T(8,128)(2,1)}), bf16[4,256,2048]{2,1,0:T(8,128)(2,1)}) %all-gather.4.cloned.1.call-update) | async-done | bytes 4194320 | tf_op jit(solution)/shard_map/all_gather | solution.py:402
  38.3 0.8 broadcast_in_dim.7.embed_ref
  39.1 18.3 %post.1 = (bf16[2048,128]{1,0:T(8,128)(2,1)}, bf16[2320,256]{1,0:T(8,128)(2,1)}, bf16[2,256,2048]{2,1,0:T(8,128)(2,1)}) custom-call(s32[2]{0:T(128)} %pad_add_fusion.ids_ref, bf16[4,256,2048]{2,1,0:T(8,128)(2,1)} %all-gather.4.cloned.1.call-done.enc_ref, f32[4,128]{1,0:T(4,128)} %bitcast.24, f32[256,128]{1,0:T(8,128)} %broadcast_in_dim.7.embed_ref, ...), custom_call_target="tpu_custom_call" | custom-call | flops 6039797760 | bytes 8388608 | tf_op jit(solution)/shard_map/post/pallas_call | solution.py:256
  57.4 22.9 %back.1 = (f32[2,4096,128]{2,1,0:T(8,128)}, bf16[2304,256]{1,0:T(8,128)(2,1)}) custom-call(bf16[2,4096,128]{2,1,0:T(8,128)(2,1)} %bitcast.28, f32[2,256,2048]{2,1,0:T(8,128)} %get-tuple-element.14.pre_ref, bf16[2,256,2048]{2,1,0:T(8,128)(2,1)} %get-tuple-element.15.eg_ref, bf16[2304,256]{1,0:T(8,128)(2,1)} %bitcast.31), custom_call_target="tpu_custom_call" | custom-call | flops 9663676416 | bytes 12582912 | tf_op jit(solution)/shard_map/back/pallas_call | solution.py:327
  80.3 1.4 slice_convert_fusion.1
  81.8 0.3 collective-permute-start.10
  82.1 0.4 collective-permute-start
  82.5 0.5 copy-done
  83.0 0.2 pad_convert_fusion
  83.2 0.1 select_convert_fusion
  83.3 0.3 collective-permute-start.20
  83.5 0.1 convert_add_fusion.2
  83.7 1.9 %collective-permute-start.11 = (bf16[288,256]{1,0:T(8,128)(2,1)S(1)}, bf16[288,256]{1,0:T(8,128)(2,1)S(1)}, u32[]{:S(2)}, u32[]{:S(2)}) collective-permute-start(bf16[288,256]{1,0:T(8,128)(2,1)S(1)} %select_convert_fusion.5), channel_id=1, source_target_pairs={{0,4},{2,6},{4,0},{6,2},{8,12},{10,14},{12,8},{14,10},{16,20},{18,... | collective-permute-start | bytes 442376 | tf_op jit(solution)/shard_map/ppermute | solution.py:363
  85.6 0.1 convert_add_fusion.3
  85.7 1.5 collective-permute-start.1
  87.3 2.6 %collective-permute-done.11 = bf16[288,256]{1,0:T(8,128)(2,1)S(1)} collective-permute-done((bf16[288,256]{1,0:T(8,128)(2,1)S(1)}, bf16[288,256]{1,0:T(8,128)(2,1)S(1)}, u32[]{:S(2)}, u32[]{:S(2)}) %collective-permute-start.11) | collective-permute-done | bytes 147488 | tf_op jit(solution)/shard_map/ppermute | solution.py:363
  89.9 1.8 %collective-permute-start.12 = (bf16[144,256]{1,0:T(8,128)(2,1)S(1)}, bf16[144,256]{1,0:T(8,128)(2,1)S(1)}, u32[]{:S(2)}, u32[]{:S(2)}) collective-permute-start(bf16[144,256]{1,0:T(8,128)(2,1)S(1)} %select_convert_fusion.8), channel_id=1, source_target_pairs={{0,2},{2,0},{4,6},{6,4},{8,10},{10,8},{12,14},{14,12},{16,18},{18,... | collective-permute-start | bytes 221192 | tf_op jit(solution)/shard_map/ppermute | solution.py:363
  91.8 1.6 collective-permute-start.2
  93.3 1.0 collective-permute-done.12
  94.4 1.8 %collective-permute-start.13 = (bf16[72,256]{1,0:T(8,128)(2,1)S(1)}, bf16[72,256]{1,0:T(8,128)(2,1)S(1)}, u32[]{:S(2)}, u32[]{:S(2)}) collective-permute-start(bf16[72,256]{1,0:T(8,128)(2,1)S(1)} %select_convert_fusion.11), channel_id=1, source_target_pairs={{0,8},{2,10},{4,12},{6,14},{8,0},{10,2},{12,4},{14,6},{16,24},{18,... | collective-permute-start | bytes 110600 | tf_op jit(solution)/shard_map/ppermute | solution.py:363
  96.2 1.6 collective-permute-start.3
  97.8 0.6 collective-permute-done.13
  98.4 2.7 %collective-permute-start.14 = (bf16[36,256]{1,0:T(8,128)(2,1)S(1)}, bf16[36,256]{1,0:T(8,128)(2,1)S(1)}, u32[]{:S(2)}, u32[]{:S(2)}) collective-permute-start(bf16[36,256]{1,0:T(8,128)(2,1)S(1)} %select_convert_fusion.13), channel_id=1, source_target_pairs={{0,16},{2,18},{4,20},{6,22},{8,24},{10,26},{12,28},{14,30},{16,0},... | collective-permute-start | bytes 55304 | tf_op jit(solution)/shard_map/ppermute | solution.py:363
  101.2 1.6 collective-permute-start.4
  102.8 0.5 collective-permute-done.14
  103.3 2.8 %collective-permute-start.15 = (bf16[36,256]{1,0:T(8,128)(2,1)S(1)}, bf16[36,256]{1,0:T(8,128)(2,1)S(1)}, u32[]{:S(2)}, u32[]{:S(2)}) collective-permute-start(bf16[36,256]{1,0:T(8,128)(2,1)S(1)} %add_convert_fusion.1), channel_id=1, source_target_pairs={{0,16},{2,18},{4,20},{6,22},{8,24},{10,26},{12,28},{14,30},{16,0},... | collective-permute-start | bytes 55304 | tf_op jit(solution)/shard_map/ppermute | solution.py:363
  106.1 1.4 collective-permute-start.5
  107.6 0.5 collective-permute-done.15
  108.0 1.9 %collective-permute-start.16 = (bf16[72,256]{1,0:T(8,128)(2,1)S(1)}, bf16[72,256]{1,0:T(8,128)(2,1)S(1)}, u32[]{:S(2)}, u32[]{:S(2)}) collective-permute-start(bf16[72,256]{1,0:T(8,128)(2,1)S(1)} %pad_maximum_fusion.13), channel_id=1, source_target_pairs={{0,8},{2,10},{4,12},{6,14},{8,0},{10,2},{12,4},{14,6},{16,24},{18,... | collective-permute-start | bytes 110600 | tf_op jit(solution)/shard_map/ppermute | solution.py:363
  109.9 0.9 collective-permute-done.5
  110.9 2.0 %collective-permute-start.6 = (bf16[72,256]{1,0:T(8,128)(2,1)S(1)}, bf16[72,256]{1,0:T(8,128)(2,1)S(1)}, u32[]{:S(2)}, u32[]{:S(2)}) collective-permute-start(bf16[72,256]{1,0:T(8,128)(2,1)S(1)} %pad_maximum_fusion.12), channel_id=1, source_target_pairs={{0,8},{2,10},{4,12},{6,14},{8,0},{10,2},{12,4},{14,6},{16,24},{18,... | collective-permute-start | bytes 110600 | tf_op jit(solution)/shard_map/ppermute | solution.py:363
  112.9 0.2 convert_add_fusion
  113.1 1.5 collective-permute-start.21
  114.7 1.4 collective-permute-start.17
  116.1 0.8 collective-permute-start.7
  116.9 4.7 %collective-permute-done.21 = bf16[584,256]{1,0:T(8,128)(2,1)S(1)} collective-permute-done((bf16[584,256]{1,0:T(8,128)(2,1)S(1)}, bf16[584,256]{1,0:T(8,128)(2,1)S(1)}, u32[]{:S(2)}, u32[]{:S(2)}) %collective-permute-start.21) | collective-permute-done | bytes 299040 | tf_op jit(solution)/shard_map/ppermute | solution.py:363
  121.5 0.1 convert_add_fusion.1
  121.7 1.4 collective-permute-start.22
  123.1 1.5 collective-permute-start.18
  124.6 3.4 %collective-permute-done.22 = bf16[292,256]{1,0:T(8,128)(2,1)S(1)} collective-permute-done((bf16[292,256]{1,0:T(8,128)(2,1)S(1)}, bf16[292,256]{1,0:T(8,128)(2,1)S(1)}, u32[]{:S(2)}, u32[]{:S(2)}) %collective-permute-start.22) | collective-permute-done | bytes 149536 | tf_op jit(solution)/shard_map/ppermute | solution.py:363
  128.2 4.3 %collective-permute-done.23 = bf16[146,256]{1,0:T(8,128)(2,1)S(1)} collective-permute-done((bf16[146,256]{1,0:T(8,128)(2,1)S(1)}, bf16[146,256]{1,0:T(8,128)(2,1)S(1)}, u32[]{:S(2)}, u32[]{:S(2)}) %collective-permute-start.23) | collective-permute-done | bytes 74784 | tf_op jit(solution)/shard_map/ppermute | solution.py:363
  132.6 1.9 %collective-permute-start.24 = (bf16[73,256]{1,0:T(8,128)(2,1)S(1)}, bf16[73,256]{1,0:T(8,128)(2,1)S(1)}, u32[]{:S(2)}, u32[]{:S(2)}) collective-permute-start(bf16[73,256]{1,0:T(8,128)(2,1)S(1)} %select_convert_fusion.10), channel_id=1, source_target_pairs={{0,16},{2,18},{4,20},{6,22},{8,24},{10,26},{12,28},{14,30},{16,0},... | collective-permute-start | bytes 112136 | tf_op jit(solution)/shard_map/ppermute | solution.py:363
  134.5 0.9 collective-permute-start.8
  135.4 2.2 %collective-permute-done.24 = bf16[73,256]{1,0:T(8,128)(2,1)S(1)} collective-permute-done((bf16[73,256]{1,0:T(8,128)(2,1)S(1)}, bf16[73,256]{1,0:T(8,128)(2,1)S(1)}, u32[]{:S(2)}, u32[]{:S(2)}) %collective-permute-start.24) | collective-permute-done | bytes 37408 | tf_op jit(solution)/shard_map/ppermute | solution.py:363
  137.6 1.9 %collective-permute-start.25 = (bf16[73,256]{1,0:T(8,128)(2,1)S(1)}, bf16[73,256]{1,0:T(8,128)(2,1)S(1)}, u32[]{:S(2)}, u32[]{:S(2)}) collective-permute-start(bf16[73,256]{1,0:T(8,128)(2,1)S(1)} %add_convert_fusion), channel_id=1, source_target_pairs={{0,16},{2,18},{4,20},{6,22},{8,24},{10,26},{12,28},{14,30},{16,0},... | collective-permute-start | bytes 112136 | tf_op jit(solution)/shard_map/ppermute | solution.py:363
  139.6 3.0 %collective-permute-done.25 = bf16[73,256]{1,0:T(8,128)(2,1)S(1)} collective-permute-done((bf16[73,256]{1,0:T(8,128)(2,1)S(1)}, bf16[73,256]{1,0:T(8,128)(2,1)S(1)}, u32[]{:S(2)}, u32[]{:S(2)}) %collective-permute-start.25) | collective-permute-done | bytes 37408 | tf_op jit(solution)/shard_map/ppermute | solution.py:363
  142.8 4.3 %collective-permute-done.26 = bf16[146,256]{1,0:T(8,128)(2,1)S(1)} collective-permute-done((bf16[146,256]{1,0:T(8,128)(2,1)S(1)}, bf16[146,256]{1,0:T(8,128)(2,1)S(1)}, u32[]{:S(2)}, u32[]{:S(2)}) %collective-permute-start.26) | collective-permute-done | bytes 74784 | tf_op jit(solution)/shard_map/ppermute | solution.py:363
  147.1 1.9 %collective-permute-start.27 = (bf16[292,256]{1,0:T(8,128)(2,1)S(1)}, bf16[292,256]{1,0:T(8,128)(2,1)S(1)}, u32[]{:S(2)}, u32[]{:S(2)}) collective-permute-start(bf16[292,256]{1,0:T(8,128)(2,1)S(1)} %pad_maximum_fusion.6), channel_id=1, source_target_pairs={{0,2},{2,0},{4,6},{6,4},{8,10},{10,8},{12,14},{14,12},{16,18},{18,... | collective-permute-start | bytes 448520 | tf_op jit(solution)/shard_map/ppermute | solution.py:363
  149.1 3.3 %collective-permute-done.27 = bf16[292,256]{1,0:T(8,128)(2,1)S(1)} collective-permute-done((bf16[292,256]{1,0:T(8,128)(2,1)S(1)}, bf16[292,256]{1,0:T(8,128)(2,1)S(1)}, u32[]{:S(2)}, u32[]{:S(2)}) %collective-permute-start.27) | collective-permute-done | bytes 149536 | tf_op jit(solution)/shard_map/ppermute | solution.py:363
  152.5 2.0 %collective-permute-start.28 = (bf16[584,256]{1,0:T(8,128)(2,1)S(1)}, bf16[584,256]{1,0:T(8,128)(2,1)S(1)}, u32[]{:S(2)}, u32[]{:S(2)}) collective-permute-start(bf16[584,256]{1,0:T(8,128)(2,1)S(1)} %pad_maximum_fusion.3), channel_id=1, source_target_pairs={{0,4},{2,6},{4,0},{6,2},{8,12},{10,14},{12,8},{14,10},{16,20},{18,... | collective-permute-start | bytes 897032 | tf_op jit(solution)/shard_map/ppermute | solution.py:363
  154.6 0.1 broadcast_select_fusion.5
  154.7 4.6 %collective-permute-done.28 = bf16[584,256]{1,0:T(8,128)(2,1)S(1)} collective-permute-done((bf16[584,256]{1,0:T(8,128)(2,1)S(1)}, bf16[584,256]{1,0:T(8,128)(2,1)S(1)}, u32[]{:S(2)}, u32[]{:S(2)}) %collective-permute-start.28) | collective-permute-done | bytes 299040 | tf_op jit(solution)/shard_map/ppermute | solution.py:363
  159.4 0.1 broadcast_select_fusion.3
  159.6 0.1 broadcast_select_fusion.7
  159.8 1.6 convert.2
  161.5 0.2 collective-permute-done.29
  161.6 0.2 broadcast_select_fusion.1
  161.8 0.2 fusion
  162.0 0.6 maximum_convert_fusion
  162.6 1.6 slice.170
  (84 shorter events, 2.0 us)
Async XLA Ops:
  7.2 15.5 %all-gather.6.cloned.1.call-start = ((), (), s32[]{:S(2)}) async-start(), calls=%async_computation.1 | async-start | bytes 1572864 | tf_op jit(solution)/shard_map/all_gather | solution.py:397
  7.9 30.4 %all-gather.4.cloned.1.call-start = ((), (), s32[]{:S(2)}) async-start(), calls=%async_computation | async-start | bytes 6291456 | tf_op jit(solution)/shard_map/all_gather | solution.py:402
  18.2 1.4 copy-start.3
  18.2 1.5 copy-start.1
  18.2 20.1 %copy-start.2 = (bf16[256]{0:T(256)(128)(2,1)S(1)}, bf16[256]{0:T(256)(128)(2,1)}, u32[]{:S(2)}) copy-start(bf16[256]{0:T(256)(128)(2,1)} %param.14) | copy-start | bytes 1540
  81.7 1.3 copy-start
  81.8 1.8 %collective-permute-start.10 = (bf16[576,256]{1,0:T(8,128)(2,1)S(1)}, bf16[576,256]{1,0:T(8,128)(2,1)S(1)}, u32[]{:S(2)}, u32[]{:S(2)}) collective-permute-start(bf16[576,256]{1,0:T(8,128)(2,1)S(1)} %select_convert_fusion.2), channel_id=1, source_target_pairs={{0,1},{1,0},{2,3},{3,2},{4,5},{5,4},{6,7},{7,6},{8,9},{9,8},{10,11... | collective-permute-start | bytes 884744 | tf_op jit(solution)/shard_map/ppermute | solution.py:363
  82.1 3.5 %collective-permute-start = (bf16[576,256]{1,0:T(8,128)(2,1)S(1)}, bf16[576,256]{1,0:T(8,128)(2,1)S(1)}, u32[]{:S(2)}, u32[]{:S(2)}) collective-permute-start(bf16[576,256]{1,0:T(8,128)(2,1)S(1)} %select_convert_fusion.3), channel_id=1, source_target_pairs={{0,1},{1,0},{2,3},{3,2},{4,5},{5,4},{6,7},{7,6},{8,9},{9,8},{10,11... | collective-permute-start | bytes 884744 | tf_op jit(solution)/shard_map/ppermute | solution.py:363
  83.3 29.6 %collective-permute-start.20 = (bf16[1168,256]{1,0:T(8,128)(2,1)S(1)}, bf16[1168,256]{1,0:T(8,128)(2,1)S(1)}, u32[]{:S(2)}, u32[]{:S(2)}) collective-permute-start(bf16[1168,256]{1,0:T(8,128)(2,1)S(1)} %select_convert_fusion), channel_id=1, source_target_pairs={{0,1},{1,0},{2,3},{3,2},{4,5},{5,4},{6,7},{7,6},{8,9},{9,8},{10,11... | collective-permute-start | bytes 1794056 | tf_op jit(solution)/shard_map/ppermute | solution.py:363
  83.7 6.1 %collective-permute-start.11 = (bf16[288,256]{1,0:T(8,128)(2,1)S(1)}, bf16[288,256]{1,0:T(8,128)(2,1)S(1)}, u32[]{:S(2)}, u32[]{:S(2)}) collective-permute-start(bf16[288,256]{1,0:T(8,128)(2,1)S(1)} %select_convert_fusion.5), channel_id=1, source_target_pairs={{0,4},{2,6},{4,0},{6,2},{8,12},{10,14},{12,8},{14,10},{16,20},{18,... | collective-permute-start | bytes 442376 | tf_op jit(solution)/shard_map/ppermute | solution.py:363
  85.7 6.0 %collective-permute-start.1 = (bf16[288,256]{1,0:T(8,128)(2,1)S(1)}, bf16[288,256]{1,0:T(8,128)(2,1)S(1)}, u32[]{:S(2)}, u32[]{:S(2)}) collective-permute-start(bf16[288,256]{1,0:T(8,128)(2,1)S(1)} %select_convert_fusion.6), channel_id=1, source_target_pairs={{0,2},{2,0},{4,6},{6,4},{8,10},{10,8},{12,14},{14,12},{16,18},{18,... | collective-permute-start | bytes 442376 | tf_op jit(solution)/shard_map/ppermute | solution.py:363
  89.9 4.4 %collective-permute-start.12 = (bf16[144,256]{1,0:T(8,128)(2,1)S(1)}, bf16[144,256]{1,0:T(8,128)(2,1)S(1)}, u32[]{:S(2)}, u32[]{:S(2)}) collective-permute-start(bf16[144,256]{1,0:T(8,128)(2,1)S(1)} %select_convert_fusion.8), channel_id=1, source_target_pairs={{0,2},{2,0},{4,6},{6,4},{8,10},{10,8},{12,14},{14,12},{16,18},{18,... | collective-permute-start | bytes 221192 | tf_op jit(solution)/shard_map/ppermute | solution.py:363
  91.8 4.4 %collective-permute-start.2 = (bf16[144,256]{1,0:T(8,128)(2,1)S(1)}, bf16[144,256]{1,0:T(8,128)(2,1)S(1)}, u32[]{:S(2)}, u32[]{:S(2)}) collective-permute-start(bf16[144,256]{1,0:T(8,128)(2,1)S(1)} %select_convert_fusion.9), channel_id=1, source_target_pairs={{0,4},{2,6},{4,0},{6,2},{8,12},{10,14},{12,8},{14,10},{16,20},{18,... | collective-permute-start | bytes 221192 | tf_op jit(solution)/shard_map/ppermute | solution.py:363
  94.4 4.0 %collective-permute-start.13 = (bf16[72,256]{1,0:T(8,128)(2,1)S(1)}, bf16[72,256]{1,0:T(8,128)(2,1)S(1)}, u32[]{:S(2)}, u32[]{:S(2)}) collective-permute-start(bf16[72,256]{1,0:T(8,128)(2,1)S(1)} %select_convert_fusion.11), channel_id=1, source_target_pairs={{0,8},{2,10},{4,12},{6,14},{8,0},{10,2},{12,4},{14,6},{16,24},{18,... | collective-permute-start | bytes 110600 | tf_op jit(solution)/shard_map/ppermute | solution.py:363
  96.2 4.9 %collective-permute-start.3 = (bf16[72,256]{1,0:T(8,128)(2,1)S(1)}, bf16[72,256]{1,0:T(8,128)(2,1)S(1)}, u32[]{:S(2)}, u32[]{:S(2)}) collective-permute-start(bf16[72,256]{1,0:T(8,128)(2,1)S(1)} %select_convert_fusion.12), channel_id=1, source_target_pairs={{0,8},{2,10},{4,12},{6,14},{8,0},{10,2},{12,4},{14,6},{16,24},{18,... | collective-permute-start | bytes 110600 | tf_op jit(solution)/shard_map/ppermute | solution.py:363
  98.4 4.8 %collective-permute-start.14 = (bf16[36,256]{1,0:T(8,128)(2,1)S(1)}, bf16[36,256]{1,0:T(8,128)(2,1)S(1)}, u32[]{:S(2)}, u32[]{:S(2)}) collective-permute-start(bf16[36,256]{1,0:T(8,128)(2,1)S(1)} %select_convert_fusion.13), channel_id=1, source_target_pairs={{0,16},{2,18},{4,20},{6,22},{8,24},{10,26},{12,28},{14,30},{16,0},... | collective-permute-start | bytes 55304 | tf_op jit(solution)/shard_map/ppermute | solution.py:363
  101.2 4.9 %collective-permute-start.4 = (bf16[36,256]{1,0:T(8,128)(2,1)S(1)}, bf16[36,256]{1,0:T(8,128)(2,1)S(1)}, u32[]{:S(2)}, u32[]{:S(2)}) collective-permute-start(bf16[36,256]{1,0:T(8,128)(2,1)S(1)} %select_convert_fusion.14), channel_id=1, source_target_pairs={{0,16},{2,18},{4,20},{6,22},{8,24},{10,26},{12,28},{14,30},{16,0},... | collective-permute-start | bytes 55304 | tf_op jit(solution)/shard_map/ppermute | solution.py:363
  103.3 4.7 %collective-permute-start.15 = (bf16[36,256]{1,0:T(8,128)(2,1)S(1)}, bf16[36,256]{1,0:T(8,128)(2,1)S(1)}, u32[]{:S(2)}, u32[]{:S(2)}) collective-permute-start(bf16[36,256]{1,0:T(8,128)(2,1)S(1)} %add_convert_fusion.1), channel_id=1, source_target_pairs={{0,16},{2,18},{4,20},{6,22},{8,24},{10,26},{12,28},{14,30},{16,0},... | collective-permute-start | bytes 55304 | tf_op jit(solution)/shard_map/ppermute | solution.py:363
  106.1 4.7 %collective-permute-start.5 = (bf16[36,256]{1,0:T(8,128)(2,1)S(1)}, bf16[36,256]{1,0:T(8,128)(2,1)S(1)}, u32[]{:S(2)}, u32[]{:S(2)}) collective-permute-start(bf16[36,256]{1,0:T(8,128)(2,1)S(1)} %add_convert_fusion.2), channel_id=1, source_target_pairs={{0,16},{2,18},{4,20},{6,22},{8,24},{10,26},{12,28},{14,30},{16,0},... | collective-permute-start | bytes 55304 | tf_op jit(solution)/shard_map/ppermute | solution.py:363
  108.0 6.6 %collective-permute-start.16 = (bf16[72,256]{1,0:T(8,128)(2,1)S(1)}, bf16[72,256]{1,0:T(8,128)(2,1)S(1)}, u32[]{:S(2)}, u32[]{:S(2)}) collective-permute-start(bf16[72,256]{1,0:T(8,128)(2,1)S(1)} %pad_maximum_fusion.13), channel_id=1, source_target_pairs={{0,8},{2,10},{4,12},{6,14},{8,0},{10,2},{12,4},{14,6},{16,24},{18,... | collective-permute-start | bytes 110600 | tf_op jit(solution)/shard_map/ppermute | solution.py:363
  110.9 5.1 %collective-permute-start.6 = (bf16[72,256]{1,0:T(8,128)(2,1)S(1)}, bf16[72,256]{1,0:T(8,128)(2,1)S(1)}, u32[]{:S(2)}, u32[]{:S(2)}) collective-permute-start(bf16[72,256]{1,0:T(8,128)(2,1)S(1)} %pad_maximum_fusion.12), channel_id=1, source_target_pairs={{0,8},{2,10},{4,12},{6,14},{8,0},{10,2},{12,4},{14,6},{16,24},{18,... | collective-permute-start | bytes 110600 | tf_op jit(solution)/shard_map/ppermute | solution.py:363
  113.1 8.4 %collective-permute-start.21 = (bf16[584,256]{1,0:T(8,128)(2,1)S(1)}, bf16[584,256]{1,0:T(8,128)(2,1)S(1)}, u32[]{:S(2)}, u32[]{:S(2)}) collective-permute-start(bf16[584,256]{1,0:T(8,128)(2,1)S(1)} %select_convert_fusion.1), channel_id=1, source_target_pairs={{0,4},{2,6},{4,0},{6,2},{8,12},{10,14},{12,8},{14,10},{16,20},{18,... | collective-permute-start | bytes 897032 | tf_op jit(solution)/shard_map/ppermute | solution.py:363
  114.7 8.4 %collective-permute-start.17 = (bf16[144,256]{1,0:T(8,128)(2,1)S(1)}, bf16[144,256]{1,0:T(8,128)(2,1)S(1)}, u32[]{:S(2)}, u32[]{:S(2)}) collective-permute-start(bf16[144,256]{1,0:T(8,128)(2,1)S(1)} %pad_maximum_fusion.11), channel_id=1, source_target_pairs={{0,2},{2,0},{4,6},{6,4},{8,10},{10,8},{12,14},{14,12},{16,18},{18,... | collective-permute-start | bytes 221192 | tf_op jit(solution)/shard_map/ppermute | solution.py:363
  116.1 12.1 %collective-permute-start.7 = (bf16[144,256]{1,0:T(8,128)(2,1)S(1)}, bf16[144,256]{1,0:T(8,128)(2,1)S(1)}, u32[]{:S(2)}, u32[]{:S(2)}) collective-permute-start(bf16[144,256]{1,0:T(8,128)(2,1)S(1)} %pad_maximum_fusion.10), channel_id=1, source_target_pairs={{0,4},{2,6},{4,0},{6,2},{8,12},{10,14},{12,8},{14,10},{16,20},{18,... | collective-permute-start | bytes 221192 | tf_op jit(solution)/shard_map/ppermute | solution.py:363
  121.7 6.3 %collective-permute-start.22 = (bf16[292,256]{1,0:T(8,128)(2,1)S(1)}, bf16[292,256]{1,0:T(8,128)(2,1)S(1)}, u32[]{:S(2)}, u32[]{:S(2)}) collective-permute-start(bf16[292,256]{1,0:T(8,128)(2,1)S(1)} %select_convert_fusion.4), channel_id=1, source_target_pairs={{0,2},{2,0},{4,6},{6,4},{8,10},{10,8},{12,14},{14,12},{16,18},{18,... | collective-permute-start | bytes 448520 | tf_op jit(solution)/shard_map/ppermute | solution.py:363
  123.1 16.4 %collective-permute-start.18 = (bf16[288,256]{1,0:T(8,128)(2,1)S(1)}, bf16[288,256]{1,0:T(8,128)(2,1)S(1)}, u32[]{:S(2)}, u32[]{:S(2)}) collective-permute-start(bf16[288,256]{1,0:T(8,128)(2,1)S(1)} %pad_maximum_fusion.8), channel_id=1, source_target_pairs={{0,4},{2,6},{4,0},{6,2},{8,12},{10,14},{12,8},{14,10},{16,20},{18,... | collective-permute-start | bytes 442376 | tf_op jit(solution)/shard_map/ppermute | solution.py:363
  128.1 4.5 %collective-permute-start.23 = (bf16[146,256]{1,0:T(8,128)(2,1)S(1)}, bf16[146,256]{1,0:T(8,128)(2,1)S(1)}, u32[]{:S(2)}, u32[]{:S(2)}) collective-permute-start(bf16[146,256]{1,0:T(8,128)(2,1)S(1)} %select_convert_fusion.7), channel_id=1, source_target_pairs={{0,8},{2,10},{4,12},{6,14},{8,0},{10,2},{12,4},{14,6},{16,24},{18,... | collective-permute-start | bytes 224264 | tf_op jit(solution)/shard_map/ppermute | solution.py:363
  132.6 5.0 %collective-permute-start.24 = (bf16[73,256]{1,0:T(8,128)(2,1)S(1)}, bf16[73,256]{1,0:T(8,128)(2,1)S(1)}, u32[]{:S(2)}, u32[]{:S(2)}) collective-permute-start(bf16[73,256]{1,0:T(8,128)(2,1)S(1)} %select_convert_fusion.10), channel_id=1, source_target_pairs={{0,16},{2,18},{4,20},{6,22},{8,24},{10,26},{12,28},{14,30},{16,0},... | collective-permute-start | bytes 112136 | tf_op jit(solution)/shard_map/ppermute | solution.py:363
  134.5 14.6 %collective-permute-start.8 = (bf16[288,256]{1,0:T(8,128)(2,1)S(1)}, bf16[288,256]{1,0:T(8,128)(2,1)S(1)}, u32[]{:S(2)}, u32[]{:S(2)}) collective-permute-start(bf16[288,256]{1,0:T(8,128)(2,1)S(1)} %pad_maximum_fusion.7), channel_id=1, source_target_pairs={{0,2},{2,0},{4,6},{6,4},{8,10},{10,8},{12,14},{14,12},{16,18},{18,... | collective-permute-start | bytes 442376 | tf_op jit(solution)/shard_map/ppermute | solution.py:363
  137.6 5.0 %collective-permute-start.25 = (bf16[73,256]{1,0:T(8,128)(2,1)S(1)}, bf16[73,256]{1,0:T(8,128)(2,1)S(1)}, u32[]{:S(2)}, u32[]{:S(2)}) collective-permute-start(bf16[73,256]{1,0:T(8,128)(2,1)S(1)} %add_convert_fusion), channel_id=1, source_target_pairs={{0,16},{2,18},{4,20},{6,22},{8,24},{10,26},{12,28},{14,30},{16,0},... | collective-permute-start | bytes 112136 | tf_op jit(solution)/shard_map/ppermute | solution.py:363
  142.6 4.5 %collective-permute-start.26 = (bf16[146,256]{1,0:T(8,128)(2,1)S(1)}, bf16[146,256]{1,0:T(8,128)(2,1)S(1)}, u32[]{:S(2)}, u32[]{:S(2)}) collective-permute-start(bf16[146,256]{1,0:T(8,128)(2,1)S(1)} %pad_maximum_fusion.9), channel_id=1, source_target_pairs={{0,8},{2,10},{4,12},{6,14},{8,0},{10,2},{12,4},{14,6},{16,24},{18,... | collective-permute-start | bytes 224264 | tf_op jit(solution)/shard_map/ppermute | solution.py:363
  142.7 11.9 %collective-permute-start.19 = (bf16[576,256]{1,0:T(8,128)(2,1)S(1)}, bf16[576,256]{1,0:T(8,128)(2,1)S(1)}, u32[]{:S(2)}, u32[]{:S(2)}) collective-permute-start(bf16[576,256]{1,0:T(8,128)(2,1)S(1)} %pad_maximum_fusion.5), channel_id=1, source_target_pairs={{0,1},{1,0},{2,3},{3,2},{4,5},{5,4},{6,7},{7,6},{8,9},{9,8},{10,11... | collective-permute-start | bytes 884744 | tf_op jit(solution)/shard_map/ppermute | solution.py:363
  147.1 5.3 %collective-permute-start.27 = (bf16[292,256]{1,0:T(8,128)(2,1)S(1)}, bf16[292,256]{1,0:T(8,128)(2,1)S(1)}, u32[]{:S(2)}, u32[]{:S(2)}) collective-permute-start(bf16[292,256]{1,0:T(8,128)(2,1)S(1)} %pad_maximum_fusion.6), channel_id=1, source_target_pairs={{0,2},{2,0},{4,6},{6,4},{8,10},{10,8},{12,14},{14,12},{16,18},{18,... | collective-permute-start | bytes 448520 | tf_op jit(solution)/shard_map/ppermute | solution.py:363
  152.5 6.8 %collective-permute-start.28 = (bf16[584,256]{1,0:T(8,128)(2,1)S(1)}, bf16[584,256]{1,0:T(8,128)(2,1)S(1)}, u32[]{:S(2)}, u32[]{:S(2)}) collective-permute-start(bf16[584,256]{1,0:T(8,128)(2,1)S(1)} %pad_maximum_fusion.3), channel_id=1, source_target_pairs={{0,4},{2,6},{4,0},{6,2},{8,12},{10,14},{12,8},{14,10},{16,20},{18,... | collective-permute-start | bytes 897032 | tf_op jit(solution)/shard_map/ppermute | solution.py:363
  154.5 5.1 %collective-permute-start.9 = (bf16[576,256]{1,0:T(8,128)(2,1)S(1)}, bf16[576,256]{1,0:T(8,128)(2,1)S(1)}, u32[]{:S(2)}, u32[]{:S(2)}) collective-permute-start(bf16[576,256]{1,0:T(8,128)(2,1)S(1)} %pad_maximum_fusion.4), channel_id=1, source_target_pairs={{0,1},{1,0},{2,3},{3,2},{4,5},{5,4},{6,7},{7,6},{8,9},{9,8},{10,11... | collective-permute-start | bytes 884744 | tf_op jit(solution)/shard_map/ppermute | solution.py:363
  159.5 2.1 %collective-permute-start.29 = (bf16[1168,256]{1,0:T(8,128)(2,1)S(1)}, bf16[1168,256]{1,0:T(8,128)(2,1)S(1)}, u32[]{:S(2)}, u32[]{:S(2)}) collective-permute-start(bf16[1168,256]{1,0:T(8,128)(2,1)S(1)} %pad_maximum_fusion.2), channel_id=1, source_target_pairs={{0,1},{1,0},{2,3},{3,2},{4,5},{5,4},{6,7},{7,6},{8,9},{9,8},{10,11... | collective-permute-start | bytes 1794056 | tf_op jit(solution)/shard_map/ppermute | solution.py:363
Sparse Core Ops, SparseCore 0:
  9.5 11.7 all-gather.5
  23.4 14.8 all-gather.3

commit v2 on v1

--- a/solution.py
+++ b/solution.py
@@ -407,12 +407,13 @@
     veh_bits = [("veh", b) for b in range(lax.axis_size("veh").bit_length() - 1)]
     one = veh_bits + scene_bits
     two = veh_bits + scene_bits[1:2] + scene_bits[:1] + scene_bits[2:]
-    post_sum = sum_over_devices(post_part, two)
     fg, enc_part = back(x, pre, eg, enc_w)
-    cut = enc_part.shape[0] // 2
-    enc_sum = jnp.concatenate(
-        [sum_over_devices(enc_part[:cut], one), sum_over_devices(enc_part[cut:], two)], axis=0
+    parts = jnp.concatenate([post_part, enc_part], axis=0)
+    cut = parts.shape[0] // 2
+    sums = jnp.concatenate(
+        [sum_over_devices(parts[:cut], one), sum_over_devices(parts[cut:], two)], axis=0
     )
+    post_sum, enc_sum = sums[: post_part.shape[0]], sums[post_part.shape[0] :]
     return (
         refined.reshape(batch, channels, half, breadth),
         fg.reshape(features.shape),

time: 171 us -> 148 us (0.87)
  waiting for transfers between devices: 52.3 us -> 37.1 us
  starting transfers between devices: 39 us -> 29.8 us
    ppermute x30 -> x20, waiting for transfers between devices: 36 us -> 20.7 us  [swap(): return lax.ppermute(x, axis, [(i, i ^ 1 << bit) for i in range(size)])]
    ppermute x30 -> x20, starting transfers between devices: 39 us -> 29.7 us  [swap(): return lax.ppermute(x, axis, [(i, i ^ 1 << bit) for i in range(size)])]
  transfers between devices with their start and end apart: 32 -> 22, of which waited for: 16 -> 14; matrix products, arithmetic and copies ran while one was open for 3% -> 4% of each run, Pallas kernels for 6% -> 23%
where the time goes in v2:
time: 148 us
  Pallas kernels  51.6 us (35%)
  waiting for transfers between devices  37.1 us (25%)
  starting transfers between devices  29.8 us (20%)
  between operations  15.7 us (11%)
  other arithmetic  7.46 us (5%)
  local copies, waits for them, and re-layouts  3.68 us (2%)
  blocking collectives  2.23 us (2%)
    ppermute x20, starting transfers between devices, swap(): return lax.ppermute(x, axis, [(i, i ^ 1 << bit) for i in range(size)])  29.7 us
    pallas_call x1, Pallas kernels, back(): pl.pallas_call(back_kernel, grid=(veh,), out_shape=(jax.ShapeDtypeStruct(...  23 us
    ppermute x20, waiting for transfers between devices, swap(): return lax.ppermute(x, axis, [(i, i ^ 1 << bit) for i in range(size)])  20.7 us
    pallas_call x1, Pallas kernels, post(): pl.pallas_call(post_kernel, out_shape=(jax.ShapeDtypeStruct((deep, LANES)...  18.3 us
    all_gather x1, waiting for transfers between devices, body(): enc_all = lax.all_gather(encoded, 'veh', axis=0, tiled=True)  15.7 us
    pallas_call x1, Pallas kernels, encode(): pl.pallas_call(encode_kernel, grid=(veh,), out_shape=(jax.ShapeDtypeStruc...  10.3 us
  transfers between devices with their start and end apart: 22, of which 14 were waited for; matrix products, arithmetic and copies ran while one was open for 4% of the time, Pallas kernels for 23%

profile of v2, /device:TPU:0, one launch (start us, length us, event | category | flops | bytes accessed | tf_op | source)
XLA Modules:
  0.0 147.5 jit_solution(17321932520764842809)
XLA Ops:
  7.2 0.7 all-gather.6.cloned.1.call-update
  7.9 10.3 %encode.1 = (f32[2,256,2048]{2,1,0:T(8,128)}, bf16[2,256,2048]{2,1,0:T(8,128)(2,1)}) custom-call(bf16[2,4096,128]{2,1,0:T(8,128)(2,1)} %bitcast.27, bf16[2304,256]{1,0:T(8,128)(2,1)} %bitcast.30), custom_call_target="tpu_custom_call" | custom-call | flops 4831838208 | bytes 8388608 | tf_op jit(solution)/shard_map/encode/pallas_call | solution.py:107
  19.6 0.1 iota_compare_fusion.1
  19.7 0.1 fusion.5
  19.8 2.2 %all-gather = f32[2,2,128]{2,1,0:T(2,128)} all-gather(f32[1,2,128]{2,1,0:T(2,128)S(1)} %bitcast.23), channel_id=1, replica_groups=mesh['scene'=16,'veh'=2] {'veh'}, dimensions={0}, use_global_device_ids=true | all-gather | bytes 3072 | tf_op jit(solution)/shard_map/all_gather | solution.py:395
  22.0 0.6 pad_add_fusion.ids_ref
  22.6 15.7 %all-gather.4.cloned.1.call-done.enc_ref = bf16[4,256,2048]{2,1,0:T(8,128)(2,1)} async-done(((bf16[2,256,2048]{2,1,0:T(8,128)(2,1)}), bf16[4,256,2048]{2,1,0:T(8,128)(2,1)}) %all-gather.4.cloned.1.call-update) | async-done | bytes 4194320 | tf_op jit(solution)/shard_map/all_gather | solution.py:402
  38.3 0.8 broadcast_in_dim.7.embed_ref
  39.1 18.3 %post.1 = (bf16[2048,128]{1,0:T(8,128)(2,1)}, bf16[2320,256]{1,0:T(8,128)(2,1)}, bf16[2,256,2048]{2,1,0:T(8,128)(2,1)}) custom-call(s32[2]{0:T(128)} %pad_add_fusion.ids_ref, bf16[4,256,2048]{2,1,0:T(8,128)(2,1)} %all-gather.4.cloned.1.call-done.enc_ref, f32[4,128]{1,0:T(4,128)} %bitcast.24, f32[256,128]{1,0:T(8,128)} %broadcast_in_dim.7.embed_ref, ...), custom_call_target="tpu_custom_call" | custom-call | flops 6039797760 | bytes 8388608 | tf_op jit(solution)/shard_map/post/pallas_call | solution.py:256
  57.4 1.3 slice.98
  58.8 0.2 pad_convert_fusion
  58.9 0.1 select_convert_fusion
  59.1 0.3 collective-permute-start.10
  59.3 23.0 %back.1 = (f32[2,4096,128]{2,1,0:T(8,128)}, bf16[2304,256]{1,0:T(8,128)(2,1)}) custom-call(bf16[2,4096,128]{2,1,0:T(8,128)(2,1)} %bitcast.28, f32[2,256,2048]{2,1,0:T(8,128)} %get-tuple-element.14.pre_ref, bf16[2,256,2048]{2,1,0:T(8,128)(2,1)} %get-tuple-element.15.eg_ref, bf16[2304,256]{1,0:T(8,128)(2,1)} %bitcast.31), custom_call_target="tpu_custom_call" | custom-call | flops 9663676416 | bytes 12582912 | tf_op jit(solution)/shard_map/back/pallas_call | solution.py:327
  82.3 1.4 fusion.3
  83.8 0.1 select_convert_fusion.1
  83.9 0.4 collective-permute-start
  84.2 0.2 convert_add_fusion
  84.5 1.8 %collective-permute-start.11 = (bf16[584,256]{1,0:T(8,128)(2,1)S(1)}, bf16[584,256]{1,0:T(8,128)(2,1)S(1)}, u32[]{:S(2)}, u32[]{:S(2)}) collective-permute-start(bf16[584,256]{1,0:T(8,128)(2,1)S(1)} %select_convert_fusion.2), channel_id=1, source_target_pairs={{0,2},{2,0},{4,6},{6,4},{8,10},{10,8},{12,14},{14,12},{16,18},{18,... | collective-permute-start | bytes 897032 | tf_op jit(solution)/shard_map/ppermute | solution.py:363
  86.3 0.2 convert_add_fusion.1
  86.6 1.6 %collective-permute-start.1 = (bf16[584,256]{1,0:T(8,128)(2,1)S(1)}, bf16[584,256]{1,0:T(8,128)(2,1)S(1)}, u32[]{:S(2)}, u32[]{:S(2)}) collective-permute-start(bf16[584,256]{1,0:T(8,128)(2,1)S(1)} %select_convert_fusion.3), channel_id=1, source_target_pairs={{0,4},{2,6},{4,0},{6,2},{8,12},{10,14},{12,8},{14,10},{16,20},{18,... | collective-permute-start | bytes 897032 | tf_op jit(solution)/shard_map/ppermute | solution.py:363
  88.1 5.8 %collective-permute-done.11 = bf16[584,256]{1,0:T(8,128)(2,1)S(1)} collective-permute-done((bf16[584,256]{1,0:T(8,128)(2,1)S(1)}, bf16[584,256]{1,0:T(8,128)(2,1)S(1)}, u32[]{:S(2)}, u32[]{:S(2)}) %collective-permute-start.11) | collective-permute-done | bytes 299040 | tf_op jit(solution)/shard_map/ppermute | solution.py:363
  93.9 0.1 convert_add_fusion.2
  94.0 1.8 %collective-permute-start.12 = (bf16[292,256]{1,0:T(8,128)(2,1)S(1)}, bf16[292,256]{1,0:T(8,128)(2,1)S(1)}, u32[]{:S(2)}, u32[]{:S(2)}) collective-permute-start(bf16[292,256]{1,0:T(8,128)(2,1)S(1)} %select_convert_fusion.4), channel_id=1, source_target_pairs={{0,4},{2,6},{4,0},{6,2},{8,12},{10,14},{12,8},{14,10},{16,20},{18,... | collective-permute-start | bytes 448520 | tf_op jit(solution)/shard_map/ppermute | solution.py:363
  95.8 0.1 convert_add_fusion.3
  96.0 1.5 %collective-permute-start.2 = (bf16[292,256]{1,0:T(8,128)(2,1)S(1)}, bf16[292,256]{1,0:T(8,128)(2,1)S(1)}, u32[]{:S(2)}, u32[]{:S(2)}) collective-permute-start(bf16[292,256]{1,0:T(8,128)(2,1)S(1)} %select_convert_fusion.5), channel_id=1, source_target_pairs={{0,2},{2,0},{4,6},{6,4},{8,10},{10,8},{12,14},{14,12},{16,18},{18,... | collective-permute-start | bytes 448520 | tf_op jit(solution)/shard_map/ppermute | solution.py:363
  97.6 1.9 %collective-permute-done.12 = bf16[292,256]{1,0:T(8,128)(2,1)S(1)} collective-permute-done((bf16[292,256]{1,0:T(8,128)(2,1)S(1)}, bf16[292,256]{1,0:T(8,128)(2,1)S(1)}, u32[]{:S(2)}, u32[]{:S(2)}) %collective-permute-start.12) | collective-permute-done | bytes 149536 | tf_op jit(solution)/shard_map/ppermute | solution.py:363
  99.4 0.1 convert_add_fusion.4
  99.6 1.8 %collective-permute-start.13 = (bf16[146,256]{1,0:T(8,128)(2,1)S(1)}, bf16[146,256]{1,0:T(8,128)(2,1)S(1)}, u32[]{:S(2)}, u32[]{:S(2)}) collective-permute-start(bf16[146,256]{1,0:T(8,128)(2,1)S(1)} %select_convert_fusion.6), channel_id=1, source_target_pairs={{0,8},{2,10},{4,12},{6,14},{8,0},{10,2},{12,4},{14,6},{16,24},{18,... | collective-permute-start | bytes 224264 | tf_op jit(solution)/shard_map/ppermute | solution.py:363
  101.5 1.5 collective-permute-start.3
  102.9 1.2 collective-permute-done.13
  104.2 2.7 %collective-permute-start.14 = (bf16[73,256]{1,0:T(8,128)(2,1)S(1)}, bf16[73,256]{1,0:T(8,128)(2,1)S(1)}, u32[]{:S(2)}, u32[]{:S(2)}) collective-permute-start(bf16[73,256]{1,0:T(8,128)(2,1)S(1)} %select_convert_fusion.8), channel_id=1, source_target_pairs={{0,16},{2,18},{4,20},{6,22},{8,24},{10,26},{12,28},{14,30},{16,0},... | collective-permute-start | bytes 112136 | tf_op jit(solution)/shard_map/ppermute | solution.py:363
  106.9 1.6 %collective-permute-start.4 = (bf16[73,256]{1,0:T(8,128)(2,1)S(1)}, bf16[73,256]{1,0:T(8,128)(2,1)S(1)}, u32[]{:S(2)}, u32[]{:S(2)}) collective-permute-start(bf16[73,256]{1,0:T(8,128)(2,1)S(1)} %select_convert_fusion.9), channel_id=1, source_target_pairs={{0,16},{2,18},{4,20},{6,22},{8,24},{10,26},{12,28},{14,30},{16,0},... | collective-permute-start | bytes 112136 | tf_op jit(solution)/shard_map/ppermute | solution.py:363
  108.5 1.0 collective-permute-done.14
  109.5 2.3 %collective-permute-start.15 = (bf16[73,256]{1,0:T(8,128)(2,1)S(1)}, bf16[73,256]{1,0:T(8,128)(2,1)S(1)}, u32[]{:S(2)}, u32[]{:S(2)}) collective-permute-start(bf16[73,256]{1,0:T(8,128)(2,1)S(1)} %add_convert_fusion), channel_id=1, source_target_pairs={{0,16},{2,18},{4,20},{6,22},{8,24},{10,26},{12,28},{14,30},{16,0},... | collective-permute-start | bytes 112136 | tf_op jit(solution)/shard_map/ppermute | solution.py:363
  111.9 0.1 collective-permute-done.4
  112.0 1.9 %collective-permute-start.5 = (bf16[73,256]{1,0:T(8,128)(2,1)S(1)}, bf16[73,256]{1,0:T(8,128)(2,1)S(1)}, u32[]{:S(2)}, u32[]{:S(2)}) collective-permute-start(bf16[73,256]{1,0:T(8,128)(2,1)S(1)} %add_convert_fusion.1), channel_id=1, source_target_pairs={{0,16},{2,18},{4,20},{6,22},{8,24},{10,26},{12,28},{14,30},{16,0},... | collective-permute-start | bytes 112136 | tf_op jit(solution)/shard_map/ppermute | solution.py:363
  113.8 0.6 collective-permute-done.15
  114.5 2.1 %collective-permute-start.16 = (bf16[146,256]{1,0:T(8,128)(2,1)S(1)}, bf16[146,256]{1,0:T(8,128)(2,1)S(1)}, u32[]{:S(2)}, u32[]{:S(2)}) collective-permute-start(bf16[146,256]{1,0:T(8,128)(2,1)S(1)} %pad_maximum_fusion.9), channel_id=1, source_target_pairs={{0,8},{2,10},{4,12},{6,14},{8,0},{10,2},{12,4},{14,6},{16,24},{18,... | collective-permute-start | bytes 224264 | tf_op jit(solution)/shard_map/ppermute | solution.py:363
  116.7 0.3 collective-permute-done.5
  117.0 2.5 %collective-permute-start.6 = (bf16[146,256]{1,0:T(8,128)(2,1)S(1)}, bf16[146,256]{1,0:T(8,128)(2,1)S(1)}, u32[]{:S(2)}, u32[]{:S(2)}) collective-permute-start(bf16[146,256]{1,0:T(8,128)(2,1)S(1)} %pad_maximum_fusion.8), channel_id=1, source_target_pairs={{0,8},{2,10},{4,12},{6,14},{8,0},{10,2},{12,4},{14,6},{16,24},{18,... | collective-permute-start | bytes 224264 | tf_op jit(solution)/shard_map/ppermute | solution.py:363
  119.6 1.5 %collective-permute-start.17 = (bf16[292,256]{1,0:T(8,128)(2,1)S(1)}, bf16[292,256]{1,0:T(8,128)(2,1)S(1)}, u32[]{:S(2)}, u32[]{:S(2)}) collective-permute-start(bf16[292,256]{1,0:T(8,128)(2,1)S(1)} %pad_maximum_fusion.7), channel_id=1, source_target_pairs={{0,4},{2,6},{4,0},{6,2},{8,12},{10,14},{12,8},{14,10},{16,20},{18,... | collective-permute-start | bytes 448520 | tf_op jit(solution)/shard_map/ppermute | solution.py:363
  121.1 0.8 collective-permute-done.6
  121.9 1.4 collective-permute-start.7
  123.4 3.0 %collective-permute-done.17 = bf16[292,256]{1,0:T(8,128)(2,1)S(1)} collective-permute-done((bf16[292,256]{1,0:T(8,128)(2,1)S(1)}, bf16[292,256]{1,0:T(8,128)(2,1)S(1)}, u32[]{:S(2)}, u32[]{:S(2)}) %collective-permute-start.17) | collective-permute-done | bytes 149536 | tf_op jit(solution)/shard_map/ppermute | solution.py:363
  126.4 0.1 broadcast_select_fusion.9
  126.5 1.4 collective-permute-start.18
  127.9 0.1 broadcast_select_fusion.11
  128.1 1.5 %collective-permute-start.8 = (bf16[584,256]{1,0:T(8,128)(2,1)S(1)}, bf16[584,256]{1,0:T(8,128)(2,1)S(1)}, u32[]{:S(2)}, u32[]{:S(2)}) collective-permute-start(bf16[584,256]{1,0:T(8,128)(2,1)S(1)} %pad_maximum_fusion.4), channel_id=1, source_target_pairs={{0,4},{2,6},{4,0},{6,2},{8,12},{10,14},{12,8},{14,10},{16,20},{18,... | collective-permute-start | bytes 897032 | tf_op jit(solution)/shard_map/ppermute | solution.py:363
  129.6 3.8 %collective-permute-done.18 = bf16[584,256]{1,0:T(8,128)(2,1)S(1)} collective-permute-done((bf16[584,256]{1,0:T(8,128)(2,1)S(1)}, bf16[584,256]{1,0:T(8,128)(2,1)S(1)}, u32[]{:S(2)}, u32[]{:S(2)}) %collective-permute-start.18) | collective-permute-done | bytes 299040 | tf_op jit(solution)/shard_map/ppermute | solution.py:363
  133.4 0.1 broadcast_select_fusion.5
  133.5 0.1 collective-permute-start.19
  133.6 1.3 collective-permute-done.8
  134.9 0.1 broadcast_select_fusion.7
  135.1 0.1 collective-permute-start.9
  135.2 0.5 collective-permute-done.19
  135.6 0.2 broadcast_select_fusion.1
  135.9 0.6 maximum_convert_fusion
  136.4 0.2 fusion.4
  136.6 0.5 collective-permute-done.9
  137.2 0.2 broadcast_select_fusion.3
  137.4 0.1 pad_maximum_fusion.1
  137.5 1.6 %convert.2 = f32[9,256,256]{2,1,0:T(8,128)} convert(bf16[9,256,256]{2,1,0:T(8,128)(2,1)S(1)} %bitcast.20) | non-fusion elementwise | flops 589824 | bytes 3538944 | tf_op jit(solution)/shard_map/reshape | solution.py:420
  139.1 1.6 %slice.132 = f32[2304,256]{1,0:T(8,128)} slice(f32[2312,256]{1,0:T(8,128)S(1)} %fusion.4), slice={[0:2304], [0:256]} | slice | bytes 4718592 | tf_op jit(solution)/shard_map/slice | solution.py:421
  (46 shorter events, 0.9 us)
Async XLA Ops:
  7.2 15.5 %all-gather.6.cloned.1.call-start = ((), (), s32[]{:S(2)}) async-start(), calls=%async_computation.1 | async-start | bytes 1572864 | tf_op jit(solution)/shard_map/all_gather | solution.py:397
  7.9 30.4 %all-gather.4.cloned.1.call-start = ((), (), s32[]{:S(2)}) async-start(), calls=%async_computation | async-start | bytes 6291456 | tf_op jit(solution)/shard_map/all_gather | solution.py:402
  18.2 1.4 copy-start.3
  18.2 1.5 %copy-start.1 = (s32[1,2,2]{2,1,0:T(2,128)S(1)}, s32[1,2,2]{2,1,0:T(2,128)}, u32[]{:S(2)}) copy-start(s32[1,2,2]{2,1,0:T(2,128)} %param.12) | copy-start | bytes 52
  18.2 20.1 %copy-start.2 = (bf16[256]{0:T(256)(128)(2,1)S(1)}, bf16[256]{0:T(256)(128)(2,1)}, u32[]{:S(2)}) copy-start(bf16[256]{0:T(256)(128)(2,1)} %param.14) | copy-start | bytes 1540
  59.1 25.2 %collective-permute-start.10 = (bf16[1168,256]{1,0:T(8,128)(2,1)S(1)}, bf16[1168,256]{1,0:T(8,128)(2,1)S(1)}, u32[]{:S(2)}, u32[]{:S(2)}) collective-permute-start(bf16[1168,256]{1,0:T(8,128)(2,1)S(1)} %select_convert_fusion), channel_id=1, source_target_pairs={{0,1},{1,0},{2,3},{3,2},{4,5},{5,4},{6,7},{7,6},{8,9},{9,8},{10,11... | collective-permute-start | bytes 1794056 | tf_op jit(solution)/shard_map/ppermute | solution.py:363
  59.3 23.0 %copy-start = (bf16[2320,256]{1,0:T(8,128)(2,1)S(1)}, bf16[2320,256]{1,0:T(8,128)(2,1)}, u32[]{:S(2)}) copy-start(bf16[2320,256]{1,0:T(8,128)(2,1)} %get-tuple-element.17) | copy-start | bytes 3563524
  83.9 2.4 %collective-permute-start = (bf16[1168,256]{1,0:T(8,128)(2,1)S(1)}, bf16[1168,256]{1,0:T(8,128)(2,1)S(1)}, u32[]{:S(2)}, u32[]{:S(2)}) collective-permute-start(bf16[1168,256]{1,0:T(8,128)(2,1)S(1)} %select_convert_fusion.1), channel_id=1, source_target_pairs={{0,1},{1,0},{2,3},{3,2},{4,5},{5,4},{6,7},{7,6},{8,9},{9,8},{10,11... | collective-permute-start | bytes 1794056 | tf_op jit(solution)/shard_map/ppermute | solution.py:363
  84.5 9.4 %collective-permute-start.11 = (bf16[584,256]{1,0:T(8,128)(2,1)S(1)}, bf16[584,256]{1,0:T(8,128)(2,1)S(1)}, u32[]{:S(2)}, u32[]{:S(2)}) collective-permute-start(bf16[584,256]{1,0:T(8,128)(2,1)S(1)} %select_convert_fusion.2), channel_id=1, source_target_pairs={{0,2},{2,0},{4,6},{6,4},{8,10},{10,8},{12,14},{14,12},{16,18},{18,... | collective-permute-start | bytes 897032 | tf_op jit(solution)/shard_map/ppermute | solution.py:363
  86.6 9.3 %collective-permute-start.1 = (bf16[584,256]{1,0:T(8,128)(2,1)S(1)}, bf16[584,256]{1,0:T(8,128)(2,1)S(1)}, u32[]{:S(2)}, u32[]{:S(2)}) collective-permute-start(bf16[584,256]{1,0:T(8,128)(2,1)S(1)} %select_convert_fusion.3), channel_id=1, source_target_pairs={{0,4},{2,6},{4,0},{6,2},{8,12},{10,14},{12,8},{14,10},{16,20},{18,... | collective-permute-start | bytes 897032 | tf_op jit(solution)/shard_map/ppermute | solution.py:363
  94.0 5.4 %collective-permute-start.12 = (bf16[292,256]{1,0:T(8,128)(2,1)S(1)}, bf16[292,256]{1,0:T(8,128)(2,1)S(1)}, u32[]{:S(2)}, u32[]{:S(2)}) collective-permute-start(bf16[292,256]{1,0:T(8,128)(2,1)S(1)} %select_convert_fusion.4), channel_id=1, source_target_pairs={{0,4},{2,6},{4,0},{6,2},{8,12},{10,14},{12,8},{14,10},{16,20},{18,... | collective-permute-start | bytes 448520 | tf_op jit(solution)/shard_map/ppermute | solution.py:363
  96.0 5.3 %collective-permute-start.2 = (bf16[292,256]{1,0:T(8,128)(2,1)S(1)}, bf16[292,256]{1,0:T(8,128)(2,1)S(1)}, u32[]{:S(2)}, u32[]{:S(2)}) collective-permute-start(bf16[292,256]{1,0:T(8,128)(2,1)S(1)} %select_convert_fusion.5), channel_id=1, source_target_pairs={{0,2},{2,0},{4,6},{6,4},{8,10},{10,8},{12,14},{14,12},{16,18},{18,... | collective-permute-start | bytes 448520 | tf_op jit(solution)/shard_map/ppermute | solution.py:363
  99.6 4.5 %collective-permute-start.13 = (bf16[146,256]{1,0:T(8,128)(2,1)S(1)}, bf16[146,256]{1,0:T(8,128)(2,1)S(1)}, u32[]{:S(2)}, u32[]{:S(2)}) collective-permute-start(bf16[146,256]{1,0:T(8,128)(2,1)S(1)} %select_convert_fusion.6), channel_id=1, source_target_pairs={{0,8},{2,10},{4,12},{6,14},{8,0},{10,2},{12,4},{14,6},{16,24},{18,... | collective-permute-start | bytes 224264 | tf_op jit(solution)/shard_map/ppermute | solution.py:363
  101.5 5.4 %collective-permute-start.3 = (bf16[146,256]{1,0:T(8,128)(2,1)S(1)}, bf16[146,256]{1,0:T(8,128)(2,1)S(1)}, u32[]{:S(2)}, u32[]{:S(2)}) collective-permute-start(bf16[146,256]{1,0:T(8,128)(2,1)S(1)} %select_convert_fusion.7), channel_id=1, source_target_pairs={{0,8},{2,10},{4,12},{6,14},{8,0},{10,2},{12,4},{14,6},{16,24},{18,... | collective-permute-start | bytes 224264 | tf_op jit(solution)/shard_map/ppermute | solution.py:363
  104.2 5.3 %collective-permute-start.14 = (bf16[73,256]{1,0:T(8,128)(2,1)S(1)}, bf16[73,256]{1,0:T(8,128)(2,1)S(1)}, u32[]{:S(2)}, u32[]{:S(2)}) collective-permute-start(bf16[73,256]{1,0:T(8,128)(2,1)S(1)} %select_convert_fusion.8), channel_id=1, source_target_pairs={{0,16},{2,18},{4,20},{6,22},{8,24},{10,26},{12,28},{14,30},{16,0},... | collective-permute-start | bytes 112136 | tf_op jit(solution)/shard_map/ppermute | solution.py:363
  106.9 5.1 %collective-permute-start.4 = (bf16[73,256]{1,0:T(8,128)(2,1)S(1)}, bf16[73,256]{1,0:T(8,128)(2,1)S(1)}, u32[]{:S(2)}, u32[]{:S(2)}) collective-permute-start(bf16[73,256]{1,0:T(8,128)(2,1)S(1)} %select_convert_fusion.9), channel_id=1, source_target_pairs={{0,16},{2,18},{4,20},{6,22},{8,24},{10,26},{12,28},{14,30},{16,0},... | collective-permute-start | bytes 112136 | tf_op jit(solution)/shard_map/ppermute | solution.py:363
  109.5 5.0 %collective-permute-start.15 = (bf16[73,256]{1,0:T(8,128)(2,1)S(1)}, bf16[73,256]{1,0:T(8,128)(2,1)S(1)}, u32[]{:S(2)}, u32[]{:S(2)}) collective-permute-start(bf16[73,256]{1,0:T(8,128)(2,1)S(1)} %add_convert_fusion), channel_id=1, source_target_pairs={{0,16},{2,18},{4,20},{6,22},{8,24},{10,26},{12,28},{14,30},{16,0},... | collective-permute-start | bytes 112136 | tf_op jit(solution)/shard_map/ppermute | solution.py:363
  112.0 5.0 %collective-permute-start.5 = (bf16[73,256]{1,0:T(8,128)(2,1)S(1)}, bf16[73,256]{1,0:T(8,128)(2,1)S(1)}, u32[]{:S(2)}, u32[]{:S(2)}) collective-permute-start(bf16[73,256]{1,0:T(8,128)(2,1)S(1)} %add_convert_fusion.1), channel_id=1, source_target_pairs={{0,16},{2,18},{4,20},{6,22},{8,24},{10,26},{12,28},{14,30},{16,0},... | collective-permute-start | bytes 112136 | tf_op jit(solution)/shard_map/ppermute | solution.py:363
  114.5 5.0 %collective-permute-start.16 = (bf16[146,256]{1,0:T(8,128)(2,1)S(1)}, bf16[146,256]{1,0:T(8,128)(2,1)S(1)}, u32[]{:S(2)}, u32[]{:S(2)}) collective-permute-start(bf16[146,256]{1,0:T(8,128)(2,1)S(1)} %pad_maximum_fusion.9), channel_id=1, source_target_pairs={{0,8},{2,10},{4,12},{6,14},{8,0},{10,2},{12,4},{14,6},{16,24},{18,... | collective-permute-start | bytes 224264 | tf_op jit(solution)/shard_map/ppermute | solution.py:363
  117.0 4.9 %collective-permute-start.6 = (bf16[146,256]{1,0:T(8,128)(2,1)S(1)}, bf16[146,256]{1,0:T(8,128)(2,1)S(1)}, u32[]{:S(2)}, u32[]{:S(2)}) collective-permute-start(bf16[146,256]{1,0:T(8,128)(2,1)S(1)} %pad_maximum_fusion.8), channel_id=1, source_target_pairs={{0,8},{2,10},{4,12},{6,14},{8,0},{10,2},{12,4},{14,6},{16,24},{18,... | collective-permute-start | bytes 224264 | tf_op jit(solution)/shard_map/ppermute | solution.py:363
  119.6 6.8 %collective-permute-start.17 = (bf16[292,256]{1,0:T(8,128)(2,1)S(1)}, bf16[292,256]{1,0:T(8,128)(2,1)S(1)}, u32[]{:S(2)}, u32[]{:S(2)}) collective-permute-start(bf16[292,256]{1,0:T(8,128)(2,1)S(1)} %pad_maximum_fusion.7), channel_id=1, source_target_pairs={{0,4},{2,6},{4,0},{6,2},{8,12},{10,14},{12,8},{14,10},{16,20},{18,... | collective-permute-start | bytes 448520 | tf_op jit(solution)/shard_map/ppermute | solution.py:363
  121.9 6.0 %collective-permute-start.7 = (bf16[292,256]{1,0:T(8,128)(2,1)S(1)}, bf16[292,256]{1,0:T(8,128)(2,1)S(1)}, u32[]{:S(2)}, u32[]{:S(2)}) collective-permute-start(bf16[292,256]{1,0:T(8,128)(2,1)S(1)} %pad_maximum_fusion.6), channel_id=1, source_target_pairs={{0,2},{2,0},{4,6},{6,4},{8,10},{10,8},{12,14},{14,12},{16,18},{18,... | collective-permute-start | bytes 448520 | tf_op jit(solution)/shard_map/ppermute | solution.py:363
  126.5 6.8 %collective-permute-start.18 = (bf16[584,256]{1,0:T(8,128)(2,1)S(1)}, bf16[584,256]{1,0:T(8,128)(2,1)S(1)}, u32[]{:S(2)}, u32[]{:S(2)}) collective-permute-start(bf16[584,256]{1,0:T(8,128)(2,1)S(1)} %pad_maximum_fusion.5), channel_id=1, source_target_pairs={{0,2},{2,0},{4,6},{6,4},{8,10},{10,8},{12,14},{14,12},{16,18},{18,... | collective-permute-start | bytes 897032 | tf_op jit(solution)/shard_map/ppermute | solution.py:363
  128.1 6.8 %collective-permute-start.8 = (bf16[584,256]{1,0:T(8,128)(2,1)S(1)}, bf16[584,256]{1,0:T(8,128)(2,1)S(1)}, u32[]{:S(2)}, u32[]{:S(2)}) collective-permute-start(bf16[584,256]{1,0:T(8,128)(2,1)S(1)} %pad_maximum_fusion.4), channel_id=1, source_target_pairs={{0,4},{2,6},{4,0},{6,2},{8,12},{10,14},{12,8},{14,10},{16,20},{18,... | collective-permute-start | bytes 897032 | tf_op jit(solution)/shard_map/ppermute | solution.py:363
  133.5 2.1 %collective-permute-start.19 = (bf16[1168,256]{1,0:T(8,128)(2,1)S(1)}, bf16[1168,256]{1,0:T(8,128)(2,1)S(1)}, u32[]{:S(2)}, u32[]{:S(2)}) collective-permute-start(bf16[1168,256]{1,0:T(8,128)(2,1)S(1)} %pad_maximum_fusion.3), channel_id=1, source_target_pairs={{0,1},{1,0},{2,3},{3,2},{4,5},{5,4},{6,7},{7,6},{8,9},{9,8},{10,11... | collective-permute-start | bytes 1794056 | tf_op jit(solution)/shard_map/ppermute | solution.py:363
  135.1 2.1 %collective-permute-start.9 = (bf16[1168,256]{1,0:T(8,128)(2,1)S(1)}, bf16[1168,256]{1,0:T(8,128)(2,1)S(1)}, u32[]{:S(2)}, u32[]{:S(2)}) collective-permute-start(bf16[1168,256]{1,0:T(8,128)(2,1)S(1)} %pad_maximum_fusion.2), channel_id=1, source_target_pairs={{0,1},{1,0},{2,3},{3,2},{4,5},{5,4},{6,7},{7,6},{8,9},{9,8},{10,11... | collective-permute-start | bytes 1794056 | tf_op jit(solution)/shard_map/ppermute | solution.py:363
Sparse Core Ops, SparseCore 0:
  9.5 11.7 all-gather.5
  23.4 14.8 all-gather.3
